TPU v7x, 32 devices: a whole 2x2x4 slice. The times are simulated.
32 devices in a mesh: seq: 16 (over z, y, x), head: 2 (over core).
Axes of the slice: x: 2, y: 2, z: 4, core: 2. Of those that a mesh axis runs over, the one named last changes fastest.
Arguments:
- block_input: bfloat16 [12, 1024, 1024], P(None, 'seq'), may hold values from -6 to 6
- seq_lengths: int32 [12], replicated, may hold values from 128 to 1024, as said below
- attn_gain: float32 [1024], replicated, may hold values from 0.5 to 1.5
- query_heads: bfloat16 [1024, 96], P(None, 'head'), may hold values from -1 to 1
- query_basis: bfloat16 [1024, 384], replicated, may hold values from -0.1875 to 0.1875
- key_heads: bfloat16 [1024, 32], P(None, 'head'), may hold values from -0.1875 to 0.1875
- key_basis: bfloat16 [1024, 128], replicated, may hold values from -0.1875 to 0.1875
- value_heads: bfloat16 [1024, 32], P(None, 'head'), may hold values from -0.1875 to 0.1875
- value_basis: bfloat16 [1024, 128], replicated, may hold values from -0.1875 to 0.1875
- out_project: bfloat16 [1024, 1024], P('head'), may hold values from -1.5 to 1.5
- ffn_gain: float32 [1024], replicated, may hold values from 0.5 to 1.5
- gate_weight: bfloat16 [1024, 2816], P(None, 'head'), may hold values from -0.1875 to 0.1875
- up_weight: bfloat16 [1024, 2816], P(None, 'head'), may hold values from -0.1875 to 0.1875
- down_weight: bfloat16 [2816, 1024], P('head'), may hold values from -0.109375 to 0.109375
- out_cotangent: bfloat16 [12, 1024, 1024], P(None, 'seq'), may hold values from -6 to 6
Outputs:
- block_output: bfloat16 [12, 1024, 1024], P(None, 'seq')
- input_grad: float32 [12, 1024, 1024], P(None, 'seq')
- attn_gain_grad: float32 [1024], replicated
- query_heads_grad: float32 [1024, 96], P(None, 'head')
- query_basis_grad: float32 [1024, 384], replicated
- key_heads_grad: float32 [1024, 32], P(None, 'head')
- key_basis_grad: float32 [1024, 128], replicated
- value_heads_grad: float32 [1024, 32], P(None, 'head')
- value_basis_grad: float32 [1024, 128], replicated
- out_project_grad: float32 [1024, 1024], P('head')
- ffn_gain_grad: float32 [1024], replicated
- gate_grad: float32 [1024, 2816], P(None, 'head')
- up_grad: float32 [1024, 2816], P(None, 'head')
- down_grad: float32 [2816, 1024], P('head')
Inputs may be any that keep to these rules, and one draw needn't show every extreme that they name: `seq_lengths`: at least one row, drawn from the seed, has the full length 1024.
All inputs are finite; a program needn't handle non-finite values.
Results may differ from a plain program's by a relative error of at most 0.025.
The roundings to bfloat16 on the way count: a program that leaves them out, or rounds other values in their place, can miss the bound.
Values may be sent and summed in bfloat16 or wider, within the bound.
A program may use at most 384 MiB of HBM per device.

v0:
```python
import math

import jax
import jax.numpy as jnp
from jax import lax
from jax.sharding import PartitionSpec as P

DH = 64
RQ = 6
RK = 2
RV = 2


highest = lax.Precision.HIGHEST
epsilon = 1e-06


def rope_angles(position):
    half_dim = DH // 2
    frequency = jnp.exp(jnp.arange(half_dim).astype(jnp.float32) * (-2.0 * math.log(10000.0) / DH))
    angles = position[:, None] * frequency[None, :]
    return (jnp.cos(angles), jnp.sin(angles))


def rotate(basis, cos_table, sin_table):
    half_dim = basis.shape[-1] // 2
    first_half = basis[..., :half_dim]
    second_half = basis[..., half_dim:]
    cos_rows = cos_table[:, None, :]
    sin_rows = sin_table[:, None, :]
    return jnp.concatenate(
        [
            first_half * cos_rows - second_half * sin_rows,
            first_half * sin_rows + second_half * cos_rows,
        ],
        axis=-1,
    )


def unrotate(basis, cos_table, sin_table):
    half_dim = basis.shape[-1] // 2
    first_half = basis[..., :half_dim]
    second_half = basis[..., half_dim:]
    cos_rows = cos_table[:, None, :]
    sin_rows = sin_table[:, None, :]
    return jnp.concatenate(
        [
            first_half * cos_rows + second_half * sin_rows,
            second_half * cos_rows - first_half * sin_rows,
        ],
        axis=-1,
    )


def rms_scale(tensor):
    return lax.rsqrt(jnp.mean(tensor * tensor, axis=-1, keepdims=True) + epsilon)


def norm_back(inputs, row_scale, gain_vec, grad_rows):
    weighted = grad_rows * gain_vec
    cubed = row_scale * row_scale * row_scale
    input_part = row_scale * weighted - inputs * cubed * jnp.mean(
        inputs * weighted, axis=-1, keepdims=True
    )
    gain_part = jnp.sum(grad_rows * inputs * row_scale, axis=(0, 1))
    return (input_part, gain_part)


def project(activations, weight):
    return jnp.einsum("rsd,de->rse", activations, weight, preferred_element_type=jnp.float32)


def back_project(grad_rows, weight):
    return jnp.einsum("rse,de->rsd", grad_rows, weight, preferred_element_type=jnp.float32)


def weight_grad(normed, grad_rows):
    return jnp.einsum("rsd,rse->de", normed, grad_rows, preferred_element_type=jnp.float32)


def split_factors(basis_part, heads_part, head_count):
    row_count, key_count = (basis_part.shape[0], basis_part.shape[1])
    key_coef = heads_part[..., : head_count * RK].reshape(row_count, key_count, head_count, RK)
    value_coef = heads_part[..., head_count * RK :].reshape(row_count, key_count, head_count, RV)
    key_vecs = basis_part[..., : RK * DH].reshape(row_count, key_count, RK, DH)
    value_vecs = basis_part[..., RK * DH :].reshape(row_count, key_count, RV, DH)
    return (key_coef, key_vecs, value_coef, value_vecs)


def rebuild(basis_part, heads_part, head_count):
    key_coef, key_vecs, value_coef, value_vecs = split_factors(basis_part, heads_part, head_count)
    key_rows = (
        jnp.einsum("rnhk,rnkd->rnhd", key_coef, key_vecs, preferred_element_type=jnp.float32) / RK
    ).astype(jnp.bfloat16)
    value_rows = (
        jnp.einsum("rnhk,rnkd->rnhd", value_coef, value_vecs, preferred_element_type=jnp.float32)
        / RV
    ).astype(jnp.bfloat16)
    return (key_rows, value_rows)


def factor_grads(d_keys, d_values, basis_part, heads_part, head_count):
    row_count, extent = (basis_part.shape[0], basis_part.shape[1])
    key_coef, key_vecs, value_coef, value_vecs = split_factors(
        basis_part.astype(jnp.float32), heads_part.astype(jnp.float32), head_count
    )
    dk_heads = jnp.einsum("rkhd,rkjd->rkhj", d_keys, key_vecs, precision=highest) / RK
    dk_basis = jnp.einsum("rkhj,rkhd->rkjd", key_coef, d_keys, precision=highest) / RK
    dv_heads = jnp.einsum("rkhd,rkjd->rkhj", d_values, value_vecs, precision=highest) / RV
    dv_basis = jnp.einsum("rkhj,rkhd->rkjd", value_coef, d_values, precision=highest) / RV
    return jnp.concatenate(
        [
            dk_basis.reshape(row_count, extent, RK * DH),
            dv_basis.reshape(row_count, extent, RV * DH),
            dk_heads.reshape(row_count, extent, head_count * RK),
            dv_heads.reshape(row_count, extent, head_count * RV),
        ],
        axis=-1,
    )


def collect(own_basis, own_heads):
    return (
        lax.all_gather(own_basis, "seq", axis=1, tiled=True),
        lax.all_gather(own_heads, "seq", axis=1, tiled=True),
    )


def masked_scores(queries, key_rows, valid_mask):
    raw_scores = jnp.einsum(
        "rqhd,rkhd->rhqk", queries, key_rows, preferred_element_type=jnp.float32
    )
    return jnp.where(valid_mask, raw_scores * (1.0 / math.sqrt(DH)), -1e30)


def shards(
    block_input,
    seq_lengths,
    attn_gain,
    query_heads,
    query_basis,
    key_heads,
    key_basis,
    value_heads,
    value_basis,
    out_project,
    ffn_gain,
    gate_weight,
    up_weight,
    down_weight,
    out_cotangent,
):
    row_count, slot_count, model_dim = block_input.shape
    head_count = query_heads.shape[1] // RQ
    length = slot_count * lax.axis_size("seq")
    first_slot = lax.axis_index("seq") * slot_count
    query_pos = first_slot + jnp.arange(slot_count, dtype=jnp.int32)
    key_pos = jnp.arange(length, dtype=jnp.int32)
    cos_table, sin_table = rope_angles(query_pos.astype(jnp.float32))
    valid_mask = (key_pos[None, None, None, :] <= query_pos[None, None, :, None]) & (
        key_pos[None, None, None, :] < seq_lengths[:, None, None, None]
    )
    score_scale = 1.0 / math.sqrt(DH)
    inputs = block_input.astype(jnp.float32)
    scale_one = rms_scale(inputs)
    normed = (inputs * scale_one * attn_gain).astype(jnp.bfloat16)
    q_heads = project(normed, query_heads).reshape(row_count, slot_count, head_count, RQ)
    q_basis = rotate(
        project(normed, query_basis).reshape(row_count, slot_count, RQ, DH), cos_table, sin_table
    )
    k_basis = (
        rotate(
            project(normed, key_basis).reshape(row_count, slot_count, RK, DH), cos_table, sin_table
        )
        .astype(jnp.bfloat16)
        .reshape(row_count, slot_count, RK * DH)
    )
    v_basis = project(normed, value_basis).astype(jnp.bfloat16)
    own_basis = jnp.concatenate([k_basis, v_basis], axis=-1)
    own_heads = jnp.concatenate(
        [project(normed, key_heads), project(normed, value_heads)], axis=-1
    ).astype(jnp.bfloat16)
    queries = (jnp.einsum("rshk,rskd->rshd", q_heads, q_basis, precision=highest) / RQ).astype(
        jnp.bfloat16
    )
    basis_all, heads_all = collect(own_basis, own_heads)
    key_rows, value_rows = rebuild(basis_all, heads_all, head_count)
    scores = masked_scores(queries, key_rows, valid_mask)
    row_peak = jnp.max(scores, axis=-1, keepdims=True)
    exp_scores = jnp.exp(scores - row_peak)
    row_total = jnp.sum(exp_scores, axis=-1, keepdims=True)
    weights_low = (exp_scores / row_total).astype(jnp.bfloat16)
    attended = jnp.einsum(
        "rhqk,rkhd->rqhd", weights_low, value_rows, preferred_element_type=jnp.float32
    )
    mixed_flat = attended.astype(jnp.bfloat16).reshape(row_count, slot_count, head_count * DH)
    attn_out = lax.psum(project(mixed_flat, out_project).astype(jnp.bfloat16), "head").astype(
        jnp.float32
    )
    middle = inputs + attn_out
    scale_two = rms_scale(middle)
    normed_two = (middle * scale_two * ffn_gain).astype(jnp.bfloat16)
    gate_act = project(normed_two, gate_weight)
    up_act = project(normed_two, up_weight)
    sigmoid_gate = jax.nn.sigmoid(gate_act)
    silu_gate = gate_act * sigmoid_gate
    hidden = (silu_gate * up_act).astype(jnp.bfloat16)
    ffn_out = lax.psum(project(hidden, down_weight).astype(jnp.bfloat16), "head").astype(
        jnp.float32
    )
    block_output = (middle + ffn_out).astype(jnp.bfloat16)
    cotangent = out_cotangent.astype(jnp.float32)
    down_grad = jnp.einsum("rsf,rsd->fd", hidden, out_cotangent, preferred_element_type=jnp.float32)
    d_hidden = jnp.einsum(
        "rsd,fd->rsf", out_cotangent, down_weight, preferred_element_type=jnp.float32
    )
    d_gate = (d_hidden * up_act * (sigmoid_gate * (1.0 + gate_act * (1.0 - sigmoid_gate)))).astype(
        jnp.bfloat16
    )
    d_up = (d_hidden * silu_gate).astype(jnp.bfloat16)
    gate_grad = jnp.einsum("rsd,rsf->df", normed_two, d_gate, preferred_element_type=jnp.float32)
    up_grad = jnp.einsum("rsd,rsf->df", normed_two, d_up, preferred_element_type=jnp.float32)
    d_normed_two = jnp.einsum(
        "rsf,df->rsd", d_gate, gate_weight, preferred_element_type=jnp.float32
    ) + jnp.einsum("rsf,df->rsd", d_up, up_weight, preferred_element_type=jnp.float32)
    d_normed_two = lax.psum(d_normed_two.astype(jnp.bfloat16), "head").astype(jnp.float32)
    d_middle_norm, ffn_gain_part = norm_back(middle, scale_two, ffn_gain, d_normed_two)
    d_middle = cotangent + d_middle_norm
    d_branch = d_middle.astype(jnp.bfloat16)
    out_project_grad = jnp.einsum(
        "rsf,rsd->fd", mixed_flat, d_branch, preferred_element_type=jnp.float32
    )
    d_mixed = (
        jnp.einsum("rsd,fd->rsf", d_branch, out_project, preferred_element_type=jnp.float32)
        .reshape(row_count, slot_count, head_count, DH)
        .astype(jnp.bfloat16)
    )
    row_delta = jnp.transpose(jnp.sum(d_mixed.astype(jnp.float32) * attended, axis=-1), (0, 2, 1))
    basis_back, heads_back = (basis_all, heads_all)
    key_back, value_back = (key_rows, value_rows)
    scores_back = masked_scores(queries, key_back, valid_mask)
    attn_weights = jnp.exp(scores_back - row_peak) / row_total
    weights_back = attn_weights.astype(jnp.bfloat16)
    d_weights = jnp.einsum(
        "rqhd,rkhd->rhqk", d_mixed, value_back, preferred_element_type=jnp.float32
    )
    d_scores = (attn_weights * (d_weights - row_delta[..., None])).astype(jnp.bfloat16)
    d_queries = (
        jnp.einsum("rhqk,rkhd->rqhd", d_scores, key_back, preferred_element_type=jnp.float32)
        * score_scale
    )
    dq_heads = jnp.einsum("rshd,rskd->rshk", d_queries, q_basis, precision=highest) / RQ
    dq_basis = unrotate(
        jnp.einsum("rshk,rshd->rskd", q_heads, d_queries, precision=highest) / RQ,
        cos_table,
        sin_table,
    )
    d_keys = (
        jnp.einsum("rhqk,rqhd->rkhd", d_scores, queries, preferred_element_type=jnp.float32)
        * score_scale
    )
    d_values = jnp.einsum(
        "rhqk,rqhd->rkhd", weights_back, d_mixed, preferred_element_type=jnp.float32
    )
    key_term = factor_grads(d_keys, d_values, basis_back, heads_back, head_count)
    key_grads = jnp.transpose(
        lax.psum_scatter(
            jnp.transpose(key_term, (1, 0, 2)).astype(jnp.bfloat16),
            "seq",
            scatter_dimension=0,
            tiled=True,
        ).astype(jnp.float32),
        (1, 0, 2),
    )
    basis_cut = (RK + RV) * DH
    dk_basis_own = (
        unrotate(
            key_grads[..., : RK * DH].reshape(row_count, slot_count, RK, DH), cos_table, sin_table
        )
        .reshape(row_count, slot_count, RK * DH)
        .astype(jnp.bfloat16)
    )
    dv_basis_own = key_grads[..., RK * DH : basis_cut].astype(jnp.bfloat16)
    dk_heads_own = key_grads[..., basis_cut : basis_cut + head_count * RK].astype(jnp.bfloat16)
    dv_heads_own = key_grads[..., basis_cut + head_count * RK :].astype(jnp.bfloat16)
    dq_heads_flat = dq_heads.reshape(row_count, slot_count, head_count * RQ).astype(jnp.bfloat16)
    dq_basis_flat = dq_basis.reshape(row_count, slot_count, RQ * DH).astype(jnp.bfloat16)
    d_normed = back_project(dq_heads_flat, query_heads) + back_project(dq_basis_flat, query_basis)
    d_normed = (
        d_normed + back_project(dk_heads_own, key_heads) + back_project(dk_basis_own, key_basis)
    )
    d_normed = (
        d_normed + back_project(dv_heads_own, value_heads) + back_project(dv_basis_own, value_basis)
    )
    d_normed = lax.psum(d_normed.astype(jnp.bfloat16), "head").astype(jnp.float32)
    d_input_norm, attn_gain_part = norm_back(inputs, scale_one, attn_gain, d_normed)
    input_grad = d_middle + d_input_norm
    query_heads_grad = weight_grad(normed, dq_heads_flat)
    query_basis_grad = weight_grad(normed, dq_basis_flat)
    key_heads_grad = weight_grad(normed, dk_heads_own)
    key_basis_grad = weight_grad(normed, dk_basis_own)
    value_heads_grad = weight_grad(normed, dv_heads_own)
    value_basis_grad = weight_grad(normed, dv_basis_own)
    (
        query_heads_grad,
        key_heads_grad,
        value_heads_grad,
        out_project_grad,
        gate_grad,
        up_grad,
        down_grad,
        attn_gain_part,
        ffn_gain_part,
    ) = (
        lax.psum(query_heads_grad.astype(jnp.bfloat16), "seq").astype(jnp.float32),
        lax.psum(key_heads_grad.astype(jnp.bfloat16), "seq").astype(jnp.float32),
        lax.psum(value_heads_grad.astype(jnp.bfloat16), "seq").astype(jnp.float32),
        lax.psum(out_project_grad.astype(jnp.bfloat16), "seq").astype(jnp.float32),
        lax.psum(gate_grad.astype(jnp.bfloat16), "seq").astype(jnp.float32),
        lax.psum(up_grad.astype(jnp.bfloat16), "seq").astype(jnp.float32),
        lax.psum(down_grad.astype(jnp.bfloat16), "seq").astype(jnp.float32),
        lax.psum(attn_gain_part.astype(jnp.bfloat16), "seq").astype(jnp.float32),
        lax.psum(ffn_gain_part.astype(jnp.bfloat16), "seq").astype(jnp.float32),
    )
    query_basis_grad, key_basis_grad, value_basis_grad = lax.psum(
        (query_basis_grad, key_basis_grad, value_basis_grad), ("seq", "head")
    )
    return (
        block_output,
        input_grad,
        attn_gain_part,
        query_heads_grad,
        query_basis_grad,
        key_heads_grad,
        key_basis_grad,
        value_heads_grad,
        value_basis_grad,
        out_project_grad,
        ffn_gain_part,
        gate_grad,
        up_grad,
        down_grad,
    )


def solution(mesh):
    in_specs = (
        P(None, "seq", None),
        P(),
        P(),
        P(None, "head"),
        P(),
        P(None, "head"),
        P(),
        P(None, "head"),
        P(),
        P("head", None),
        P(),
        P(None, "head"),
        P(None, "head"),
        P("head", None),
        P(None, "seq", None),
    )
    out_specs = (
        P(None, "seq", None),
        P(None, "seq", None),
        P(),
        P(None, "head"),
        P(),
        P(None, "head"),
        P(),
        P(None, "head"),
        P(),
        P("head", None),
        P(),
        P(None, "head"),
        P(None, "head"),
        P("head", None),
    )
    return jax.shard_map(shards, mesh=mesh, in_specs=in_specs, out_specs=out_specs, check_vma=False)
```

profile of v0, /device:TPU:0, one launch (start us, length us, event | category | flops | bytes accessed | tf_op | source)
XLA Modules:
  0.0 1774.2 jit_solution(7163479684345712720)
XLA Ops:
  31.0 3.7 fusion.54
  34.8 3.2 reshape.252
  40.2 4.1 multiply_subtract_fusion
  46.9 8.0 multiply_convert_fusion.13
  57.8 124.6 %all_gather.6 = bf16[12,1024,32]{2,0,1:T(8,128)(2,1)S(1)} all-gather(bf16[12,64,32]{2,0,1:T(8,128)(2,1)S(1)} %copy.174), channel_id=1, replica_groups=mesh['seq'=16,'head'=2] {'seq'}, dimensions={1}, use_global_device_ids=true | all-gather | bytes 835584 | tf_op jit(solution)/shard_map/all_gather | solution.py:125
  182.4 4.3 fusion.100
  186.7 5.0 copy.175
  192.8 5.0 copy.181
  199.7 14.4 copy.183
  214.1 10.8 copy.177
  226.4 6.2 fusion.99
  232.5 4.6 copy.176
  237.2 15.5 copy.178
  252.7 4.6 copy.182
  257.3 15.6 copy.184
  272.9 23.0 %fusion.103 = f32[12,1024,8,64]{3,2,1,0:T(8,128)} fusion(bf16[12,1024,8,2]{2,3,1,0:T(2,128)(2,1)} %copy.177, bf16[12,1024,2,64]{3,2,1,0:T(2,128)(2,1)} %copy.178), kind=kOutput, calls=%fused_computation.166 | convolution fusion | flops 25165824 | bytes 28704768 | tf_op jit(solution)/shard_map/rnhk,rnkd->rnhd/dot_general | solution.py:96
  295.9 36.4 %copy.179 = f32[12,1024,8,64]{1,3,2,0:T(8,128)} copy(f32[12,1024,8,64]{3,2,1,0:T(8,128)} %fusion.103) | data formatting | bytes 50331648 | tf_op jit(solution)/shard_map/rnhk,rnkd->rnhd/dot_general | solution.py:96
  332.4 23.0 %fusion.104 = f32[12,1024,8,64]{3,2,1,0:T(8,128)} fusion(bf16[12,1024,8,2]{2,3,1,0:T(2,128)(2,1)} %copy.183, bf16[12,1024,2,64]{3,2,1,0:T(2,128)(2,1)} %copy.184), kind=kOutput, calls=%fused_computation.167 | convolution fusion | flops 25165824 | bytes 28704768 | tf_op jit(solution)/shard_map/rnhk,rnkd->rnhd/dot_general | solution.py:93
  355.4 36.5 %copy.185 = f32[12,1024,8,64]{1,3,2,0:T(8,128)} copy(f32[12,1024,8,64]{3,2,1,0:T(8,128)} %fusion.104) | data formatting | bytes 50331648 | tf_op jit(solution)/shard_map/rnhk,rnkd->rnhd/dot_general | solution.py:93
  391.9 16.9 fusion.8
  408.8 32.9 %fusion.102 = (f32[12,8,64]{2,1,0:T(8,128)S(1)}, f32[12,8,64,1024]{3,2,1,0:T(8,128)}) fusion(f32[12,8,64,1024]{3,2,1,0:T(8,128)} %fusion.8, pred[12,64,1024]{2,1,0:T(8,128)(4,1)} %broadcast_and_fusion), kind=kOutput, calls=%fused_computation.165 | output fusion | flops 37749760 | bytes 51142656 | tf_op jit(solution)/shard_map/sub | solution.py:190
  441.8 14.0 fusion.5
  455.8 15.8 bitcast_convert_fusion.3
  471.6 3.9 convolution_convert_fusion
  475.5 7.0 fusion.28
  482.5 17.4 all-reduce.11.cloned.1.call-done
  507.0 5.7 multiply_convert_fusion.10
  515.4 3.8 add_convert_fusion.2
  519.2 21.7 %all-reduce.13.cloned.1.call-done = bf16[12,64,1024]{2,1,0:T(8,128)(2,1)} async-done(((bf16[12,64,1024]{2,1,0:T(8,128)(2,1)}), bf16[12,64,1024]{2,1,0:T(8,128)(2,1)}) %all-reduce.13.cloned.1.call-update) | async-done | bytes 1572880 | tf_op jit(solution)/shard_map/psum | solution.py:226
  540.9 4.5 fusion.19
  553.0 16.9 convolution_bitcast_fusion
  569.9 33.9 %copy.200 = f32[12,1024,8,64]{3,2,1,0:T(8,128)} copy(f32[12,1024,8,64]{1,3,2,0:T(8,128)} %convolution_bitcast_fusion) | data formatting | bytes 50331648 | tf_op jit(solution)/shard_map/rhqk,rqhd->rkhd/transpose | solution.py:262
  603.8 45.7 %fusion.108 = f32[12,1024,8,2]{2,3,1,0:T(2,128)} fusion(f32[12,1024,8,64]{3,2,1,0:T(8,128)} %copy.200, bf16[12,1024,2,64]{3,2,1,0:T(2,128)(2,1)} %copy.178), kind=kOutput, calls=%fused_computation.171 | convolution fusion | flops 150994944 | bytes 29097984 | tf_op jit(solution)/shard_map/rkhd,rkjd->rkhj/dot_general | solution.py:109
  649.5 45.2 %fusion.106 = f32[12,1024,2,64]{3,2,1,0:T(2,128)} fusion(bf16[12,1024,8,2]{2,3,1,0:T(2,128)(2,1)} %copy.177, f32[12,1024,8,64]{3,2,1,0:T(8,128)} %copy.200), kind=kOutput, calls=%fused_computation.169 | convolution fusion | flops 150994944 | bytes 31850496 | tf_op jit(solution)/shard_map/rkhj,rkhd->rkjd/dot_general | solution.py:110
  697.2 22.8 %multiply_convert_fusion = bf16[12,8,64,1024]{3,2,1,0:T(8,128)(2,1)} fusion(f32[12,8,64]{2,1,0:T(8,128)S(1)} %bitcast.180, f32[12,8,64,1024]{3,2,1,0:T(8,128)} %get-tuple-element.58, f32[12,8,64]{2,1,0:T(8,128)S(1)} %get-tuple-element.57, bf16[12,64,8,64]{1,3,2,0:T(8,128)(2,1)} %bitcast.165, f32[12,1024,8,64]{1,3,2,0:T(8,128)} %copy.179), kind=kOutput, calls=%fused_computation.2 | convolution fusion | flops 843055104 | bytes 63750144 | tf_op jit(solution)/shard_map/rqhd,rkhd->rhqk/dot_general | solution.py:244
  720.1 16.3 multiply_bitcast_fusion
  736.4 33.9 %copy.197 = f32[12,1024,8,64]{3,2,1,0:T(8,128)} copy(f32[12,1024,8,64]{1,3,2,0:T(8,128)} %multiply_bitcast_fusion) | data formatting | bytes 50331648 | tf_op jit(solution)/shard_map/mul | solution.py:259
  770.3 45.9 %fusion.107 = f32[12,1024,8,2]{2,3,1,0:T(2,128)} fusion(f32[12,1024,8,64]{3,2,1,0:T(8,128)} %copy.197, bf16[12,1024,2,64]{3,2,1,0:T(2,128)(2,1)} %copy.184), kind=kOutput, calls=%fused_computation.170 | convolution fusion | flops 150994944 | bytes 29097984 | tf_op jit(solution)/shard_map/rkhd,rkjd->rkhj/dot_general | solution.py:107
  816.2 45.0 %fusion.105 = f32[12,1024,2,64]{3,2,1,0:T(2,128)} fusion(bf16[12,1024,8,2]{2,3,1,0:T(2,128)(2,1)} %copy.183, f32[12,1024,8,64]{3,2,1,0:T(8,128)} %copy.197), kind=kOutput, calls=%fused_computation.168 | convolution fusion | flops 150994944 | bytes 31850496 | tf_op jit(solution)/shard_map/rkhj,rkhd->rkjd/dot_general | solution.py:108
  861.2 15.1 copy.208
  876.3 17.7 copy.201
  894.0 5.4 multiply_convert_fusion.3
  900.0 15.1 copy.204
  915.1 17.7 copy.198
  932.8 5.4 multiply_convert_fusion.4
  938.8 6.1 maximum_bitcast_fusion
  944.9 15.7 copy.210
  962.5 5.7 fusion.40
  968.2 16.0 multiply_bitcast_fusion.1
  984.2 3.6 copy.190
  987.8 11.6 fusion.51
  1001.9 7.5 convolution_multiply_fusion
  1020.4 145.6 %reduce-scatter.2.cloned.1.call-done = bf16[64,12,288]{2,1,0:T(8,128)(2,1)} async-done(((bf16[1024,12,288]{2,1,0:T(8,128)(2,1)}), bf16[64,12,288]{2,1,0:T(8,128)(2,1)}) %reduce-scatter.2.cloned.1.call-update) | async-done | bytes 442384 | tf_op jit(solution)/shard_map/reduce_scatter | solution.py:267
  1177.4 7.0 add_convert_fusion
  1185.7 5.8 bitcast_convert_fusion
  1191.5 4.0 bitcast_convert_fusion.2
  1195.6 4.0 bitcast_convert_fusion.1
  1209.6 3.3 fusion.26
  1214.8 293.2 %all-reduce.19.cloned.1.call-done = (bf16[1024,48]{0,1:T(8,128)(2,1)}, bf16[512,1024]{1,0:T(8,128)(2,1)}, bf16[1024,1408]{1,0:T(8,128)(2,1)}, bf16[1024,1408]{1,0:T(8,128)(2,1)}, bf16[1408,1024]{1,0:T(8,128)(2,1)}) async-done(((bf16[1024,48]{0,1:T(8,128)(2,1)}, bf16[512,1024]{1,0:T(8,128)(2,1)}, bf16[1024,1408]{1,0:T(8,128)(2,1)}, bf16[1024,1408]{1,0:T(8,128)(2,1)}, bf16[1408,1024]{1,0:T(8,128)(2,1)}), ...) | async-done | bytes 9797648 | tf_op jit(solution)/shard_map/psum | solution.py:315
  1515.6 3.3 convert_element_type.230
  1519.0 3.7 convert_element_type.232
  1524.5 4.0 fusion.14
  1528.5 90.2 %all-reduce.17.cloned.1.call-done = (bf16[1024]{0:T(1024)(128)(2,1)}, bf16[1024,16]{0,1:T(8,128)(2,1)}, bf16[1024,16]{0,1:T(8,128)(2,1)}, bf16[1024]{0:T(1024)(128)(2,1)}) async-done(((bf16[1024]{0:T(1024)(128)(2,1)}, bf16[1024,16]{0,1:T(8,128)(2,1)}, bf16[1024,16]{0,1:T(8,128)(2,1)}, bf16[1024]{0:T(1024)(128)(2,1)}), (bf16[1024]{0:T(1024)(128)(2,1)}, bf16[1024,16]{0,1:T(8,128)(2,1)}, ...) | async-done | bytes 69648 | tf_op jit(solution)/shard_map/psum | solution.py:322
  1624.0 138.7 %all-reduce.15.cloned.1.call-done = (f32[1024,384]{1,0:T(8,128)}, f32[1024,128]{1,0:T(8,128)}, f32[1024,128]{1,0:T(8,128)}) async-done(((f32[1024,384]{1,0:T(8,128)}, f32[1024,128]{1,0:T(8,128)}, f32[1024,128]{1,0:T(8,128)}), (f32[1024,384]{1,0:T(8,128)}, f32[1024,128]{1,0:T(8,128)}, f32[1024,128]{1,0:T(8,128)})) %all-reduce.15.cloned.1.call-update) | async-done | bytes 2621456 | tf_op jit(solution)/shard_map/psum | solution.py:325
  (234 shorter events, 116.0 us)
Async XLA Ops:
  7.2 499.8 %copy-start = (bf16[1024,1408]{1,0:T(8,128)(2,1)S(1)}, bf16[1024,1408]{1,0:T(8,128)(2,1)}, u32[]{:S(2)}) copy-start(bf16[1024,1408]{1,0:T(8,128)(2,1)} %param.26) | copy-start | bytes 8650756
  7.2 6.3 copy-start.57
  7.2 6.2 copy-start.39
  7.2 219.2 %all-gather.2.cloned.1.call-start = ((), (), s32[]{:S(2)}) async-start(), calls=%async_computation.1 | async-start | bytes 6684672 | tf_op jit(solution)/shard_map/all_gather | solution.py:124
  7.8 5.7 copy-start.2
  10.7 20.3 %copy-start.44 = (f32[12,64]{1,0:T(8,128)}, f32[12,64]{1,0:T(8,128)S(1)}, u32[]{:S(2)}) copy-start(f32[12,64]{1,0:T(8,128)S(1)} %get-tuple-element.52) | copy-start | bytes 9220
  14.1 8.1 copy-start.52
  18.9 5.5 copy-start.54
  22.0 5.0 copy-start.42
  22.0 477.9 %all-reduce.11.cloned.1.call-start = ((), (), s32[]{:S(2)}) async-start(), calls=%async_computation.2 | async-start | bytes 3145728 | tf_op jit(solution)/shard_map/psum | solution.py:197
  40.2 6.8 copy-start.9
  214.1 10.8 copy-start.59
  475.4 65.4 %all-reduce.13.cloned.1.call-start = ((), (), s32[]{:S(2)}) async-start(), calls=%async_computation.3 | async-start | bytes 3145728 | tf_op jit(solution)/shard_map/psum | solution.py:226
  482.5 20.1 %copy-start.50 = (f32[1024]{0:T(1024)S(1)}, f32[1024]{0:T(1024)}, u32[]{:S(2)}) copy-start(f32[1024]{0:T(1024)} %param.25) | copy-start | bytes 12292
  499.9 2.7 copy-start.3
  499.9 2.8 copy-start.7
  502.5 42.8 %copy-start.40 = (f32[12,64]{1,0:T(8,128)}, f32[12,64]{1,0:T(8,128)S(1)}, u32[]{:S(2)}) copy-start(f32[12,64]{1,0:T(8,128)S(1)} %get-tuple-element.54) | copy-start | bytes 9220
  502.5 42.8 %copy-start.46 = (f32[12,64]{1,0:T(8,128)}, f32[12,64]{1,0:T(8,128)S(1)}, u32[]{:S(2)}) copy-start(f32[12,64]{1,0:T(8,128)S(1)} %get-tuple-element.53) | copy-start | bytes 9220
  502.7 4.3 slice-start
  519.1 26.2 %copy-start.4 = (bf16[12,64,1024]{2,1,0:T(8,128)(2,1)S(1)}, bf16[12,64,1024]{2,1,0:T(8,128)(2,1)}, u32[]{:S(2)}) copy-start(bf16[12,64,1024]{2,1,0:T(8,128)(2,1)} %param.15) | copy-start | bytes 4718596
  519.2 646.8 %reduce-scatter.2.cloned.1.call-start = ((), (), s32[]{:S(2)}) async-start(), calls=%async_computation.4 | async-start | bytes 13369344 | tf_op jit(solution)/shard_map/reduce_scatter | solution.py:267
  540.9 4.5 copy-start.14
  545.3 2.8 copy-start.48
  545.4 4.0 copy-start.28
  553.0 141.6 %copy-start.13 = (bf16[12,64,512]{1,2,0:T(8,128)(2,1)}, bf16[12,64,512]{1,2,0:T(8,128)(2,1)S(1)}, u32[]{:S(2)}) copy-start(bf16[12,64,512]{1,2,0:T(8,128)(2,1)S(1)} %copy.188) | copy-start | bytes 2359300
  697.2 22.8 %copy-start.12 = (bf16[12,64,8,64]{1,3,2,0:T(8,128)(2,1)S(1)}, bf16[12,64,8,64]{1,3,2,0:T(8,128)(2,1)}, u32[]{:S(2)}) copy-start(bf16[12,64,8,64]{1,3,2,0:T(8,128)(2,1)} %copy.195) | copy-start | bytes 2359300
  960.7 248.9 %all-reduce.21.cloned.1.call-start = ((), (), s32[]{:S(2)}) async-start(), calls=%async_computation.8 | async-start | bytes 6291456 | tf_op jit(solution)/shard_map/psum | solution.py:208
  1001.9 7.5 copy-start.30
  1001.9 7.5 copy-start.32
  1012.7 2.7 copy-start.43
  1012.7 5.0 copy-start.33
  1015.4 4.9 copy-start.34
  1017.7 150.4 %copy-start.53 = (bf16[1024,16]{0,1:T(8,128)(2,1)S(1)}, bf16[1024,16]{0,1:T(8,128)(2,1)}, u32[]{:S(2)}) copy-start(bf16[1024,16]{0,1:T(8,128)(2,1)} %param.22) | copy-start | bytes 98308
  1020.4 149.9 %copy-start.55 = (bf16[1024,16]{0,1:T(8,128)(2,1)S(1)}, bf16[1024,16]{0,1:T(8,128)(2,1)}, u32[]{:S(2)}) copy-start(bf16[1024,16]{0,1:T(8,128)(2,1)} %param.20) | copy-start | bytes 98308
  1174.5 2.8 copy-start.38
  1184.4 323.7 %all-reduce.19.cloned.1.call-start = ((), (), s32[]{:S(2)}) async-start(), calls=%async_computation.7 | async-start | bytes 19595264 | tf_op jit(solution)/shard_map/psum | solution.py:315
  1185.7 5.8 copy-start.24
  1185.7 5.8 copy-start.63
  1191.5 4.0 copy-start.65
  1195.6 4.1 copy-start.5
  1195.6 4.1 copy-start.35
  1195.6 4.1 copy-start.45
  1195.6 4.1 copy-start.58
  1195.6 5.3 copy-start.16
  1195.6 5.3 copy-start.26
  1202.9 415.8 %all-reduce.17.cloned.1.call-start = ((), (), s32[]{:S(2)}) async-start(), calls=%async_computation.6 | async-start | bytes 139264 | tf_op jit(solution)/shard_map/psum | solution.py:322
  1212.9 549.8 %all-reduce.15.cloned.1.call-start = ((), (), s32[]{:S(2)}) async-start(), calls=%async_computation.5 | async-start | bytes 5242880 | tf_op jit(solution)/shard_map/psum | solution.py:325
  1508.0 4.5 copy-start.22
  1512.6 3.0 copy-start.21
  1515.6 3.3 copy-start.20
  1515.6 7.0 copy-start.27
  1518.9 3.7 copy-start.6
  1518.9 3.7 copy-start.8
  1518.9 4.3 copy-start.15
  1518.9 5.1 copy-start.18
  1518.9 5.5 copy-start.19
  1518.9 5.5 copy-start.41
  1518.9 5.5 copy-start.47
  1518.9 5.5 copy-start.49
  1518.9 5.5 copy-start.51
  1519.0 5.5 copy-start.56
  1524.5 242.6 %copy-start.1 = (bf16[1024,1408]{1,0:T(8,128)(2,1)S(1)}, bf16[1024,1408]{1,0:T(8,128)(2,1)}, u32[]{:S(2)}) copy-start(bf16[1024,1408]{1,0:T(8,128)(2,1)} %param.26) | copy-start | bytes 8650756
  1762.8 2.7 copy-start.37
  1762.8 3.5 copy-start.36
  (12 other events, 26.3 us)
Sparse Core Ops, SparseCore 0:
  22.1 125.2 all-gather.1
  475.6 24.2 all-reduce.10
  519.3 21.5 all-reduce.12
  960.8 205.1 reduce-scatter.1
  1184.5 22.8 all-reduce.20
  1214.8 293.1 all-reduce.18
  1515.1 103.5 all-reduce.16
  1625.6 137.1 all-reduce.14
where the time goes:
time: 1790 us; the launch traced here: 1770 us
  waiting for transfers between devices  707 us (39%)
  matrix products  450 us (25%)
  local copies, waits for them, and re-layouts  351 us (20%)
  blocking collectives  125 us (7%)
  other arithmetic  124 us (7%)
    psum x1, waiting for transfers between devices, shards(): lax.psum(query_heads_grad.astype(jnp.bfloat16), 'seq').astype(jnp.float32)  293 us
    reduce_scatter x1, waiting for transfers between devices, shards(): lax.psum_scatter(jnp.transpose(key_term, (1, 0, 2)).astype(jnp.bfloat16),...  146 us
    psum x1, waiting for transfers between devices, shards(): lax.psum((query_basis_grad, key_basis_grad, value_basis_grad), ('seq', 'h...  139 us
    all_gather x1, blocking collectives, collect(): lax.all_gather(own_heads, 'seq', axis=1, tiled=True)  125 us
    psum x1, waiting for transfers between devices, shards(): lax.psum(attn_gain_part.astype(jnp.bfloat16), 'seq').astype(jnp.float32)  90.2 us
    dot_general x1, matrix products, factor_grads(): jnp.einsum('rkhd,rkjd->rkhj', d_keys, key_vecs, precision=highest) / RK  45.9 us
    dot_general x1, matrix products, factor_grads(): jnp.einsum('rkhd,rkjd->rkhj', d_values, value_vecs, precision=highest) / RV  45.7 us
    dot_general x1, matrix products, factor_grads(): jnp.einsum('rkhj,rkhd->rkjd', value_coef, d_values, precision=highest) / RV  45.2 us
  transfers between devices with their start and end apart: 8, of which 6 were waited for; matrix products, arithmetic and copies ran while one was open for 11% of the time, Pallas kernels for 0%

commit v1 on v0

v1 whole, which is shorter than its diff:
```python
import functools
import math

import jax
import jax.numpy as jnp
from jax import lax
from jax.experimental import pallas as pl
from jax.experimental.pallas import tpu as pltpu
from jax.sharding import PartitionSpec as P

DH = 64
RQ = 6
RK = 2
RV = 2
LANES = 128
EPS = 1e-06
KEY_BLOCK = 256
F32 = jnp.float32
BF16 = jnp.bfloat16


def dot(a, b):
    return lax.dot_general(a, b, (((1,), (0,)), ((), ())), preferred_element_type=F32)


def dot_nt(a, b):
    return lax.dot_general(a, b, (((1,), (1,)), ((), ())), preferred_element_type=F32)


def dot_tn(a, b):
    return lax.dot_general(a, b, (((0,), (0,)), ((), ())), preferred_element_type=F32)


def lane_of(shape):
    return lax.broadcasted_iota(jnp.int32, shape, len(shape) - 1)


def both_halves(pair):
    swapped = pltpu.roll(pair, DH, 1)
    low = lane_of(pair.shape) < DH
    return jnp.where(low, pair, swapped), jnp.where(low, swapped, pair)


def turn(pair, cos, sin):
    half = DH // 2
    first = lane_of(pair.shape) % DH < half
    other = jnp.where(first, pltpu.roll(pair, LANES - half, 1), pltpu.roll(pair, half, 1))
    return pair * cos + other * sin


def split_heads(rows, head_rows, tokens):
    group = lane_of(rows.shape) // DH
    return jnp.concatenate([jnp.where(group == h, rows, jnp.zeros_like(rows)) for h in range(head_rows)], axis=0)


def join_heads(block, head_rows, tokens):
    out = block[:tokens]
    group = lane_of(out.shape) // DH
    for h in range(1, head_rows):
        out = jnp.where(group == h, block[h * tokens : (h + 1) * tokens], out)
    return out


def factor_kernel(width, x_ref, gain_ref, wqh_ref, wqb_ref, wkb_ref, wvb_ref, wh_ref, cos_ref, sin_ref, eq_ref,
                  xn_ref, aq_ref, bq_ref, q_ref, kv_ref, hd_ref):
    rows, tokens, model = x_ref.shape
    hd = q_ref.shape[2]
    count = rows * tokens
    x = x_ref[...].astype(F32).reshape(count, model)
    scale = lax.rsqrt(jnp.mean(x * x, axis=-1, keepdims=True) + EPS)
    xn = (x * scale * gain_ref[...]).astype(BF16)
    xn_ref[...] = xn.reshape(rows, tokens, model)
    cos = jnp.concatenate([cos_ref[...]] * rows, axis=0)
    sin = jnp.concatenate([sin_ref[...]] * rows, axis=0)
    keys = turn(dot(xn, wkb_ref[...]), cos, sin).astype(BF16)
    values = dot(xn, wvb_ref[...]).astype(BF16)
    heads = dot(xn, wh_ref[...])
    lanes = lane_of((tokens, LANES)) // width
    pack = heads[:tokens]
    for r in range(rows):
        part = slice(r * tokens, (r + 1) * tokens)
        kv_ref[2 * r] = keys[part]
        kv_ref[2 * r + 1] = values[part]
        if r:
            pack = jnp.where(lanes == r, heads[part], pack)
    hd_ref[0] = pack.astype(BF16)
    aq = dot(xn, wqh_ref[...])
    aq_ref[...] = aq.reshape(rows, tokens, aq.shape[1])
    aq_high = aq.astype(BF16)
    aq_low = (aq - aq_high.astype(F32)).astype(BF16)
    basis = dot(xn, wqb_ref[...])
    total = [jnp.zeros((count, LANES), F32) for _ in range(hd // LANES)]
    for p in range(RQ // 2):
        pair = turn(basis[:, p * LANES : (p + 1) * LANES], cos, sin)
        bq_ref[:, :, p * LANES : (p + 1) * LANES] = pair.reshape(rows, tokens, LANES)
        for half, vec in enumerate(both_halves(pair)):
            spread = eq_ref[:, (2 * p + half) * hd : (2 * p + half + 1) * hd]
            coef = dot(aq_high, spread) + dot(aq_low, spread)
            for c in range(hd // LANES):
                total[c] = total[c] + coef[:, c * LANES : (c + 1) * LANES] * vec
    for c in range(hd // LANES):
        low = (total[c] / RQ).astype(BF16).astype(F32) * (1.0 / math.sqrt(DH))
        q_ref[:, :, c * LANES : (c + 1) * LANES] = low.astype(BF16).reshape(rows, tokens, LANES)


def whole(*shape):
    return pl.BlockSpec(shape, lambda *_: (0,) * len(shape))


def factors(x, gain, wqh, wqb, wkb, wvb, wh, cos, sin, eq, pack_rows, width):
    rows, tokens, model = x.shape
    hd = eq.shape[1] // RQ
    packs = rows // pack_rows
    nq = wqh.shape[1]

    def row_block(last):
        return pl.BlockSpec((pack_rows, tokens, last), lambda g: (g, 0, 0))

    return pl.pallas_call(
        functools.partial(factor_kernel, width),
        grid=(packs,),
        in_specs=[row_block(model), whole(1, model), whole(*wqh.shape), whole(*wqb.shape), whole(*wkb.shape),
                  whole(*wvb.shape), whole(*wh.shape), whole(*cos.shape), whole(*sin.shape), whole(*eq.shape)],
        out_specs=[row_block(model), row_block(nq), row_block(RQ * DH), row_block(hd),
                   pl.BlockSpec((2 * pack_rows, tokens, LANES), lambda g: (g, 0, 0)),
                   pl.BlockSpec((1, tokens, LANES), lambda g: (g, 0, 0))],
        out_shape=[
            jax.ShapeDtypeStruct((rows, tokens, model), BF16),
            jax.ShapeDtypeStruct((rows, tokens, nq), F32),
            jax.ShapeDtypeStruct((rows, tokens, RQ * DH), F32),
            jax.ShapeDtypeStruct((rows, tokens, hd), BF16),
            jax.ShapeDtypeStruct((2 * rows, tokens, LANES), BF16),
            jax.ShapeDtypeStruct((packs, tokens, LANES), BF16),
        ],
        compiler_params=pltpu.CompilerParams(vmem_limit_bytes=56 * 2**20),
        name="factors",
    )(x, gain.reshape(1, model), wqh, wqb, wkb, wvb, wh, cos, sin, eq)


def query_grad_kernel(dq_ref, aq_ref, bq_ref, eq_ref, cos_ref, sin_ref, da_ref, db_ref):
    rows, tokens, hd = dq_ref.shape
    count = rows * tokens
    dq = dq_ref[...].reshape(count, hd)
    aq = aq_ref[...].reshape(count, aq_ref.shape[2])
    aq_high = aq.astype(BF16)
    aq_low = (aq - aq_high.astype(F32)).astype(BF16)
    cos = jnp.concatenate([cos_ref[...]] * rows, axis=0)
    sin = jnp.concatenate([sin_ref[...]] * rows, axis=0)
    da = jnp.zeros(aq.shape, F32)
    low = lane_of((count, LANES)) < DH
    for p in range(RQ // 2):
        pair = bq_ref[:, :, p * LANES : (p + 1) * LANES].reshape(count, LANES)
        sums = []
        for half, vec in enumerate(both_halves(pair)):
            spread = eq_ref[:, (2 * p + half) * hd : (2 * p + half + 1) * hd]
            coef = dot(aq_high, spread) + dot(aq_low, spread)
            acc = jnp.zeros((count, LANES), F32)
            prods = []
            for c in range(hd // LANES):
                part = dq[:, c * LANES : (c + 1) * LANES]
                acc = acc + coef[:, c * LANES : (c + 1) * LANES] * part
                prods.append(part * vec)
            prod = jnp.concatenate(prods, axis=1)
            high = prod.astype(BF16)
            rest = (prod - high.astype(F32)).astype(BF16)
            da = da + dot_nt(high, spread) + dot_nt(rest, spread)
            sums.append(acc + pltpu.roll(acc, DH, 1))
        turned = turn(jnp.where(low, sums[0], sums[1]), cos, -sin) * (1.0 / RQ)
        db_ref[:, :, p * LANES : (p + 1) * LANES] = turned.astype(BF16).reshape(rows, tokens, LANES)
    da_ref[...] = (da * (1.0 / RQ)).astype(BF16).reshape(da_ref.shape)


def query_grads(dq, aq, bq, eq, cos, sin, pack_rows):
    rows, tokens, hd = dq.shape
    nq = aq.shape[2]

    def row_block(last):
        return pl.BlockSpec((pack_rows, tokens, last), lambda g: (g, 0, 0))

    return pl.pallas_call(
        query_grad_kernel,
        grid=(rows // pack_rows,),
        in_specs=[row_block(hd), row_block(nq), row_block(RQ * DH), whole(*eq.shape), whole(*cos.shape), whole(*sin.shape)],
        out_specs=[row_block(nq), row_block(RQ * DH)],
        out_shape=[jax.ShapeDtypeStruct((rows, tokens, nq), BF16), jax.ShapeDtypeStruct((rows, tokens, RQ * DH), BF16)],
        compiler_params=pltpu.CompilerParams(vmem_limit_bytes=56 * 2**20),
        name="query_grads",
    )(dq, aq, bq, eq, cos, sin)


def build_rows(basis, coefs, spread, hd):
    first, second = both_halves(basis.astype(F32))
    coef = dot(coefs, spread)
    one, two = coef[:, :hd], coef[:, hd:]
    cols = [one[:, c : c + LANES] * first + two[:, c : c + LANES] * second for c in range(0, hd, LANES)]
    return jnp.concatenate(cols, axis=1).astype(BF16), one, two, first, second


def row_limits(info_ref, row, tokens, block):
    first = info_ref[info_ref.shape[0] - 1]
    length = info_ref[row]
    used = jnp.minimum(length, first + tokens)
    return first, length, (used + block - 1) // block


def limit_lanes(first, length, tokens, lanes):
    slot = lax.broadcasted_iota(jnp.int32, (1, lanes), 1) % tokens
    return jnp.minimum(first + slot, length - 1)


def attend_kernel(pack_rows, group, block, info_ref, q_ref, kv_ref, hd_ref, spread_ref, o_ref, ob_ref, lse_ref, s_ref, v_ref):
    row = pl.program_id(0)
    _, tokens, hd = q_ref.shape
    lanes = group * tokens
    wide = group * DH
    groups = hd // wide
    first, length, blocks = row_limits(info_ref, row, tokens, block)
    limit = limit_lanes(first, length, tokens, lanes)
    queries = [split_heads(q_ref[0, :, g * wide : (g + 1) * wide], group, tokens) for g in range(groups)]
    place = row % pack_rows

    def scores(b, peaks):
        at = pl.ds(pl.multiple_of(b * block, block), block)
        coefs = hd_ref[0, at, :]
        keys, *_ = build_rows(kv_ref[0, at, :], coefs, spread_ref[place, :, : 2 * hd], hd)
        values, *_ = build_rows(kv_ref[1, at, :], coefs, spread_ref[place, :, 2 * hd :], hd)
        position = b * block + lax.broadcasted_iota(jnp.int32, (block, 1), 0)
        live = position < first + tokens
        v_ref[at, :] = jnp.where(live, values.astype(F32), 0.0).astype(BF16)
        out = []
        for g in range(groups):
            raw = dot_nt(keys[:, g * wide : (g + 1) * wide], queries[g])
            raw = jnp.where(position <= limit, raw, -1e30)
            s_ref[at, g * lanes : (g + 1) * lanes] = raw
            out.append(jnp.maximum(peaks[g], jnp.max(raw, axis=0, keepdims=True)))
        return tuple(out)

    peaks = lax.fori_loop(0, blocks, scores, tuple(jnp.full((1, lanes), -1e30, F32) for _ in range(groups)))

    def exps(b, totals):
        at = pl.ds(pl.multiple_of(b * block, block), block)
        out = []
        for g in range(groups):
            part = slice(g * lanes, (g + 1) * lanes)
            e = jnp.exp(s_ref[at, part] - peaks[g])
            s_ref[at, part] = e
            out.append(totals[g] + jnp.sum(e, axis=0, keepdims=True))
        return tuple(out)

    totals = lax.fori_loop(0, blocks, exps, tuple(jnp.zeros((1, lanes), F32) for _ in range(groups)))
    shares = [1.0 / t for t in totals]

    def mix(b, outs):
        at = pl.ds(pl.multiple_of(b * block, block), block)
        res = []
        for g in range(groups):
            p = (s_ref[at, g * lanes : (g + 1) * lanes] * shares[g]).astype(BF16)
            res.append(outs[g] + dot_tn(p, v_ref[at, g * wide : (g + 1) * wide]))
        return tuple(res)

    outs = lax.fori_loop(0, blocks, mix, tuple(jnp.zeros((lanes, wide), F32) for _ in range(groups)))
    for g in range(groups):
        mixed = join_heads(outs[g], group, tokens)
        o_ref[0, :, g * wide : (g + 1) * wide] = mixed
        ob_ref[0, :, g * wide : (g + 1) * wide] = mixed.astype(BF16)
        lse_ref[0, :, g * lanes : (g + 1) * lanes] = peaks[g] + jnp.log(totals[g])


def attend(info, q, kv, shift, spread, pack_rows, group, block):
    rows, tokens, hd = q.shape
    length = kv.shape[1]
    n_lanes = hd // DH * tokens
    grid_spec = pltpu.PrefetchScalarGridSpec(
        num_scalar_prefetch=1,
        grid=(rows,),
        in_specs=[
            pl.BlockSpec((1, tokens, hd), lambda r, i: (r, 0, 0)),
            pl.BlockSpec((2, length, LANES), lambda r, i: (lax.rem(r + i[rows], rows), 0, 0)),
            pl.BlockSpec((1, length, LANES), lambda r, i: (2 * rows + r // pack_rows, 0, 0)),
            pl.BlockSpec(spread.shape, lambda r, i: (0, 0, 0)),
        ],
        out_specs=[
            pl.BlockSpec((1, tokens, hd), lambda r, i: (r, 0, 0)),
            pl.BlockSpec((1, tokens, hd), lambda r, i: (r, 0, 0)),
            pl.BlockSpec((1, 1, n_lanes), lambda r, i: (r, 0, 0)),
        ],
        scratch_shapes=[pltpu.VMEM((length, n_lanes), F32), pltpu.VMEM((length, hd), BF16)],
    )
    return pl.pallas_call(
        functools.partial(attend_kernel, pack_rows, group, block),
        grid_spec=grid_spec,
        out_shape=[
            jax.ShapeDtypeStruct((rows, tokens, hd), F32),
            jax.ShapeDtypeStruct((rows, tokens, hd), BF16),
            jax.ShapeDtypeStruct((rows, 1, n_lanes), F32),
        ],
        compiler_params=pltpu.CompilerParams(vmem_limit_bytes=56 * 2**20),
        name="attend",
    )(info, q, kv, kv, spread)


def attend_back_kernel(pack_rows, group, block, info_ref, q_ref, kv_ref, hd_ref, spread_ref, o_ref, do_ref, lse_ref,
                       dq_ref, dkv_ref, dhd_ref, dq_acc):
    row = pl.program_id(0)
    _, tokens, hd = q_ref.shape
    lanes = group * tokens
    wide = group * DH
    groups = hd // wide
    first, length, blocks = row_limits(info_ref, row, tokens, block)
    limit = limit_lanes(first, length, tokens, lanes)
    place = row % pack_rows
    queries, grads, deltas, peaks = [], [], [], []
    for g in range(groups):
        part = slice(g * wide, (g + 1) * wide)
        do = do_ref[0, :, part]
        queries.append(split_heads(q_ref[0, :, part], group, tokens))
        grads.append(split_heads(do, group, tokens))
        weighed = split_heads(do.astype(F32) * o_ref[0, :, part], group, tokens)
        high = weighed.astype(BF16)
        low = (weighed - high.astype(F32)).astype(BF16)
        ones = jnp.ones((16, wide), BF16)
        deltas.append((dot_nt(ones, high) + dot_nt(ones, low))[:1])
        peaks.append(lse_ref[0, :, g * lanes : (g + 1) * lanes])
    dq_acc[...] = jnp.zeros_like(dq_acc)
    dkv_ref[...] = jnp.zeros_like(dkv_ref)

    @pl.when(place == 0)
    def _():
        dhd_ref[...] = jnp.zeros_like(dhd_ref)

    def fold(coef, grad):
        acc = coef[:, :LANES] * grad[:, :LANES]
        for c in range(LANES, hd, LANES):
            acc = acc + coef[:, c : c + LANES] * grad[:, c : c + LANES]
        return acc + pltpu.roll(acc, DH, 1)

    def times(grad, vec):
        return jnp.concatenate([grad[:, c : c + LANES] * vec for c in range(0, hd, LANES)], axis=1).astype(BF16)

    def one(b, carry):
        at = pl.ds(pl.multiple_of(b * block, block), block)
        position = b * block + lax.broadcasted_iota(jnp.int32, (block, 1), 0)
        live = position < first + tokens
        coefs = jnp.where(live, hd_ref[0, at, :].astype(F32), 0.0).astype(BF16)
        kbasis = jnp.where(live, kv_ref[0, at, :].astype(F32), 0.0)
        vbasis = jnp.where(live, kv_ref[1, at, :].astype(F32), 0.0)
        keys, ka, kb, k0, k1 = build_rows(kbasis, coefs, spread_ref[place, :, : 2 * hd], hd)
        values, va, vb, v0, v1 = build_rows(vbasis, coefs, spread_ref[place, :, 2 * hd :], hd)
        dks, dvs = [], []
        for g in range(groups):
            part = slice(g * wide, (g + 1) * wide)
            raw = dot_nt(keys[:, part], queries[g])
            p = jnp.where(position <= limit, jnp.exp(raw - peaks[g]), 0.0)
            dp = dot_nt(values[:, part], grads[g])
            ds = (p * (dp - deltas[g])).astype(BF16)
            dvs.append(dot(p.astype(BF16), grads[g]))
            dks.append(dot(ds, queries[g]))
            dq_acc[g] += dot_tn(ds, keys[:, part])
        dk = jnp.concatenate(dks, axis=1)
        dv = jnp.concatenate(dvs, axis=1)
        low = lane_of((block, LANES)) < DH
        dkv_ref[0, at, :] = jnp.where(low, fold(ka, dk), fold(kb, dk)).astype(BF16)
        dkv_ref[1, at, :] = jnp.where(low, fold(va, dv), fold(vb, dv)).astype(BF16)
        prods = jnp.concatenate([times(dk, k0), times(dk, k1), times(dv, v0), times(dv, v1)], axis=1)
        dcoef = dot_nt(prods, spread_ref[place])
        dhd_ref[0, at, :] = (dhd_ref[0, at, :].astype(F32) + dcoef).astype(BF16)
        return carry

    lax.fori_loop(0, blocks, one, 0)
    for g in range(groups):
        dq_ref[0, :, g * wide : (g + 1) * wide] = join_heads(dq_acc[g], group, tokens) * (1.0 / math.sqrt(DH))


def attend_back(info, q, kv, spread, o, do, lse, pack_rows, group, block):
    rows, tokens, hd = q.shape
    length = kv.shape[1]
    n_lanes = hd // DH * tokens
    packs = rows // pack_rows

    def place(r, i):
        return (lax.rem(r + i[rows], rows), 0, 0)

    def own(r, i):
        return (r, 0, 0)

    grid_spec = pltpu.PrefetchScalarGridSpec(
        num_scalar_prefetch=1,
        grid=(rows,),
        in_specs=[
            pl.BlockSpec((1, tokens, hd), own),
            pl.BlockSpec((2, length, LANES), place),
            pl.BlockSpec((1, length, LANES), lambda r, i: (2 * rows + r // pack_rows, 0, 0)),
            pl.BlockSpec(spread.shape, lambda r, i: (0, 0, 0)),
            pl.BlockSpec((1, tokens, hd), own),
            pl.BlockSpec((1, tokens, hd), own),
            pl.BlockSpec((1, 1, n_lanes), own),
        ],
        out_specs=[
            pl.BlockSpec((1, tokens, hd), own),
            pl.BlockSpec((2, length, LANES), place),
            pl.BlockSpec((1, length, LANES), lambda r, i: (r // pack_rows, 0, 0)),
        ],
        scratch_shapes=[pltpu.VMEM((hd // (group * DH), group * tokens, group * DH), F32)],
    )
    return pl.pallas_call(
        functools.partial(attend_back_kernel, pack_rows, group, block),
        grid_spec=grid_spec,
        out_shape=[
            jax.ShapeDtypeStruct((rows, tokens, hd), F32),
            jax.ShapeDtypeStruct((2 * rows, length, LANES), BF16),
            jax.ShapeDtypeStruct((packs, length, LANES), BF16),
        ],
        compiler_params=pltpu.CompilerParams(vmem_limit_bytes=56 * 2**20),
        name="attend_back",
    )(info, q, kv, kv, spread, o, do, lse)


def norm_back(inputs, row_scale, gain_vec, grad_rows):
    weighted = grad_rows * gain_vec
    cubed = row_scale * row_scale * row_scale
    input_part = row_scale * weighted - inputs * cubed * jnp.mean(inputs * weighted, axis=-1, keepdims=True)
    gain_part = jnp.sum(grad_rows * inputs * row_scale, axis=(0, 1))
    return (input_part, gain_part)


def project(activations, weight):
    return jnp.einsum("rsd,de->rse", activations, weight, preferred_element_type=F32)


def back_project(grad_rows, weight):
    return jnp.einsum("rse,de->rsd", grad_rows, weight, preferred_element_type=F32)


def weight_grad(normed, grad_rows):
    return jnp.einsum("rsd,rse->de", normed, grad_rows, preferred_element_type=F32)


def head_sum(partial):
    return lax.psum(partial.astype(BF16), "head").astype(F32)


def rms_scale(tensor):
    return lax.rsqrt(jnp.mean(tensor * tensor, axis=-1, keepdims=True) + EPS)


def spread_tables(head_count, width, pack_rows):
    hd = head_count * DH
    lane = jnp.arange(LANES, dtype=jnp.int32)[None, :, None]
    row = jnp.arange(pack_rows, dtype=jnp.int32)[:, None, None]
    col = jnp.arange(4 * hd, dtype=jnp.int32)[None, None, :]
    kind, head = col // hd, col % hd // DH
    source = row * width + (kind // 2) * (head_count * RK) + head * RK + kind % 2
    spread = jnp.where(lane == source, 0.5, 0.0).astype(BF16)
    factor = jnp.arange(head_count * RQ, dtype=jnp.int32)[:, None]
    col = jnp.arange(RQ * hd, dtype=jnp.int32)[None, :]
    query = jnp.where(factor == col % hd // DH * RQ + col // hd, 1.0, 0.0).astype(BF16)
    return spread, query


def rope_tables(position):
    half = DH // 2
    frequency = jnp.exp(jnp.arange(half).astype(F32) * (-2.0 * math.log(10000.0) / DH))
    angles = position[:, None] * frequency[None, :]
    cos, sin = jnp.cos(angles), jnp.sin(angles)
    return jnp.concatenate([cos] * 4, axis=1), jnp.concatenate([-sin, sin, -sin, sin], axis=1)


def shards(
    block_input,
    seq_lengths,
    attn_gain,
    query_heads,
    query_basis,
    key_heads,
    key_basis,
    value_heads,
    value_basis,
    out_project,
    ffn_gain,
    gate_weight,
    up_weight,
    down_weight,
    out_cotangent,
):
    row_count, slot_count, model_dim = block_input.shape
    head_count = query_heads.shape[1] // RQ
    hd = head_count * DH
    length = slot_count * lax.axis_size("seq")
    first_slot = lax.axis_index("seq") * slot_count
    width = head_count * (RK + RV)
    pack_rows = max(n for n in range(1, row_count + 1) if row_count % n == 0 and n * width <= LANES)
    group = min(4, head_count)
    block = math.gcd(length, KEY_BLOCK)
    spread, query_spread = spread_tables(head_count, width, pack_rows)
    cos, sin = rope_tables((first_slot + jnp.arange(slot_count, dtype=jnp.int32)).astype(F32))
    both = jnp.concatenate([key_heads, value_heads], axis=1)
    packed = jnp.concatenate([both] * pack_rows + [jnp.zeros((model_dim, LANES - width * pack_rows), BF16)], axis=1)
    normed, aq, bq, queries, own_kv, own_heads = factors(
        block_input, attn_gain, query_heads, query_basis, key_basis, value_basis, packed, cos, sin, query_spread,
        pack_rows, width)
    inputs = block_input.astype(F32)
    scale_one = rms_scale(inputs)
    kv = lax.all_gather(jnp.concatenate([own_kv, own_heads], axis=0), "seq", axis=1, tiled=True)
    shift = jnp.zeros((), jnp.int32)
    info = jnp.stack([*[seq_lengths[r] for r in range(row_count)], shift, first_slot]).astype(jnp.int32)
    attended, mixed_flat, lse = attend(info, queries, kv, shift, spread, pack_rows, group, block)
    attn_out = head_sum(project(mixed_flat, out_project))
    middle = inputs + attn_out
    scale_two = rms_scale(middle)
    normed_two = (middle * scale_two * ffn_gain).astype(BF16)
    gate_act = project(normed_two, gate_weight)
    up_act = project(normed_two, up_weight)
    sigmoid_gate = jax.nn.sigmoid(gate_act)
    silu_gate = gate_act * sigmoid_gate
    hidden = (silu_gate * up_act).astype(BF16)
    ffn_out = head_sum(project(hidden, down_weight))
    block_output = (middle + ffn_out).astype(BF16)
    cotangent = out_cotangent.astype(F32)
    down_grad = jnp.einsum("rsf,rsd->fd", hidden, out_cotangent, preferred_element_type=F32)
    d_hidden = jnp.einsum("rsd,fd->rsf", out_cotangent, down_weight, preferred_element_type=F32)
    d_gate = (d_hidden * up_act * (sigmoid_gate * (1.0 + gate_act * (1.0 - sigmoid_gate)))).astype(BF16)
    d_up = (d_hidden * silu_gate).astype(BF16)
    gate_grad = weight_grad(normed_two, d_gate)
    up_grad = weight_grad(normed_two, d_up)
    d_normed_two = head_sum(back_project(d_gate, gate_weight) + back_project(d_up, up_weight))
    d_middle_norm, ffn_gain_part = norm_back(middle, scale_two, ffn_gain, d_normed_two)
    d_middle = cotangent + d_middle_norm
    d_branch = d_middle.astype(BF16)
    out_project_grad = jnp.einsum("rsf,rsd->fd", mixed_flat, d_branch, preferred_element_type=F32)
    d_mixed = back_project(d_branch, out_project).astype(BF16)
    d_queries, d_kv, d_heads = attend_back(info, queries, kv, spread, attended, d_mixed, lse, pack_rows, group, block)
    dq_heads, dq_basis = query_grads(d_queries, aq, bq, query_spread, cos, sin, pack_rows)
    key_grads = lax.psum_scatter(
        jnp.concatenate([d_kv, d_heads], axis=0), "seq", scatter_dimension=1, tiled=True)
    d_kv_own = key_grads[: 2 * row_count].reshape(row_count, 2, slot_count, LANES).astype(F32)
    half = DH // 2
    pairs = d_kv_own[:, 0].reshape(row_count, slot_count, 2, 2, half)
    u, w = pairs[:, :, :, 0], pairs[:, :, :, 1]
    c, s = cos[None, :, None, :half], sin[None, :, None, half:DH]
    dk_basis = jnp.stack([u * c + w * s, w * c - u * s], axis=3).reshape(row_count, slot_count, LANES).astype(BF16)
    dv_basis = d_kv_own[:, 1].astype(BF16)
    packs = row_count // pack_rows
    d_heads_own = key_grads[2 * row_count :, :, : width * pack_rows].reshape(packs, slot_count, pack_rows, width)
    d_heads_own = jnp.transpose(d_heads_own, (0, 2, 1, 3)).reshape(row_count, slot_count, width).astype(BF16)
    dk_heads, dv_heads = d_heads_own[..., : head_count * RK], d_heads_own[..., head_count * RK :]
    d_normed = head_sum(
        back_project(dq_heads, query_heads) + back_project(dq_basis, query_basis)
        + back_project(dk_heads, key_heads) + back_project(dk_basis, key_basis)
        + back_project(dv_heads, value_heads) + back_project(dv_basis, value_basis))
    d_input_norm, attn_gain_part = norm_back(inputs, scale_one, attn_gain, d_normed)
    input_grad = d_middle + d_input_norm
    head_grads = weight_grad(normed, jnp.concatenate([dq_heads, dk_heads, dv_heads], axis=-1))
    basis_grads = weight_grad(normed, jnp.concatenate([dq_basis, dk_basis, dv_basis], axis=-1))

    def seq_sum(*parts):
        return tuple(t.astype(F32) for t in lax.psum(tuple(t.astype(BF16) for t in parts), "seq"))

    gate_grad, up_grad, down_grad = seq_sum(gate_grad, up_grad, down_grad)
    out_project_grad, head_grads, attn_gain_part, ffn_gain_part = seq_sum(
        out_project_grad, head_grads, attn_gain_part, ffn_gain_part)
    basis_grads = lax.psum(basis_grads, ("seq", "head"))
    nq, nk = head_count * RQ, head_count * RK
    return (
        block_output,
        input_grad,
        attn_gain_part,
        head_grads[:, :nq],
        basis_grads[:, : RQ * DH],
        head_grads[:, nq : nq + nk],
        basis_grads[:, RQ * DH : (RQ + RK) * DH],
        head_grads[:, nq + nk :],
        basis_grads[:, (RQ + RK) * DH :],
        out_project_grad,
        ffn_gain_part,
        gate_grad,
        up_grad,
        down_grad,
    )


def solution(mesh):
    rows = P(None, "seq", None)
    columns, features = P(None, "head"), P("head", None)
    in_specs = (rows, P(), P(), columns, P(), columns, P(), columns, P(), features, P(), columns, columns, features, rows)
    out_specs = (rows, rows, P(), columns, P(), columns, P(), columns, P(), features, P(), columns, columns, features)
    return jax.shard_map(shards, mesh=mesh, in_specs=in_specs, out_specs=out_specs, check_vma=False)
```

time: 1790 us -> 949 us (0.53)
  matrix products: 450 us -> 64.4 us
  local copies, waits for them, and re-layouts: 351 us -> 22.9 us
  blocking collectives: 125 us -> 43.5 us
  other arithmetic: 124 us -> 44.9 us
  Pallas kernels: 0 us -> 61.1 us
  waiting for transfers between devices: 707 us -> 685 us
    dot_general x44 -> x19, matrix products: 444 us -> 57.4 us  [the longest x9 18.1 us: back_project(): jnp.einsum('rse,de->rsd', grad_rows, weight, preferred_element_type=F32)]
    dot_general x7 -> x0, local copies, waits for them, and re-layouts: 141 us -> none  [the longest x1 36.5 us: rebuild(): jnp.einsum('rnhk,rnkd->rnhd', key_coef, key_vecs, preferred_element_type=...]
    psum x6 -> x5, waiting for transfers between devices: 561 us -> 430 us  [the longest x1 251 us: seq_sum(): lax.psum(tuple((t.astype(BF16) for t in parts)), 'seq')]
    all_gather x1 -> x0, blocking collectives: 125 us -> none  [collect(): lax.all_gather(own_heads, 'seq', axis=1, tiled=True)]
    all_gather x1, waiting for transfers between devices: 0.01 us -> 103 us  [shards(): lax.all_gather(jnp.concatenate([own_kv, own_heads], axis=0), 'seq', axis=...]
    reshape x12 -> x0, local copies, waits for them, and re-layouts: 67.4 us -> none  [the longest x2 16.3 us: split_factors(): heads_part[..., :head_count * RK]]
    pallas_call x0 -> x4, Pallas kernels: none -> 61.1 us  [the longest x1 27.5 us: attend_back(): pl.pallas_call(functools.partial(attend_back_kernel, pack_rows, group, bl...]
    psum x0 -> x1, blocking collectives: none -> 43.5 us  [seq_sum(): lax.psum(tuple((t.astype(BF16) for t in parts)), 'seq')]
  transfers between devices with their start and end apart: 8 -> 7, of which waited for: 6 -> 7; matrix products, arithmetic and copies ran while one was open for 11% -> 6% of each run, Pallas kernels for 0% -> 1%
where the time goes in v1:
time: 949 us; the launch traced here: 938 us
  waiting for transfers between devices  685 us (72%)
  matrix products  64.4 us (7%)
  Pallas kernels  61.1 us (6%)
  other arithmetic  44.9 us (5%)
  blocking collectives  43.5 us (5%)
  local copies, waits for them, and re-layouts  22.9 us (2%)
  between operations  14.8 us (2%)
    psum x1, waiting for transfers between devices, seq_sum(): lax.psum(tuple((t.astype(BF16) for t in parts)), 'seq')  251 us
    reduce_scatter x1, waiting for transfers between devices, shards(): lax.psum_scatter(jnp.concatenate([d_kv, d_heads], axis=0), 'seq', scatter...  151 us
    psum x1, waiting for transfers between devices, shards(): basis_grads = lax.psum(basis_grads, ('seq', 'head'))  114 us
    all_gather x1, waiting for transfers between devices, shards(): lax.all_gather(jnp.concatenate([own_kv, own_heads], axis=0), 'seq', axis=...  103 us
    psum x3, waiting for transfers between devices, head_sum(): return lax.psum(partial.astype(BF16), 'head').astype(F32)  65.9 us
    psum x1, blocking collectives, seq_sum(): lax.psum(tuple((t.astype(BF16) for t in parts)), 'seq')  43.5 us
    pallas_call x1, Pallas kernels, attend_back(): pl.pallas_call(functools.partial(attend_back_kernel, pack_rows, group, bl...  27.5 us
  transfers between devices with their start and end apart: 7, of which 7 were waited for; matrix products, arithmetic and copies ran while one was open for 6% of the time, Pallas kernels for 1%

profile of v1, /device:TPU:0, one launch (start us, length us, event | category | flops | bytes accessed | tf_op | source)
XLA Modules:
  0.0 937.7 jit_solution(7101765398625085012)
XLA Ops:
  7.3 1.9 copy.109.wqh_ref
  9.2 0.9 copy.100
  10.1 0.9 copy.101
  11.0 0.8 select_convert_fusion.1.eq_ref
  12.0 3.9 concatenate.27.wh_ref
  15.9 0.7 pad_maximum_fusion.4
  16.7 8.5 factors.1
  25.1 1.8 pad_maximum_fusion.1
  27.1 0.6 pad_add_fusion.info_ref
  27.8 1.9 select_convert_fusion.spread_ref
  29.6 102.9 %all-gather.2.cloned.1.call-done.kv_ref.hd_ref = bf16[27,1024,128]{2,1,0:T(8,128)(2,1)} async-done(((bf16[27,64,128]{2,1,0:T(8,128)(2,1)}), bf16[27,1024,128]{2,1,0:T(8,128)(2,1)}) %all-gather.2.cloned.1.call-update) | async-done | bytes 7077904 | tf_op jit(solution)/shard_map/all_gather | solution.py:503
  132.5 17.2 %attend.1 = (f32[12,64,512]{2,1,0:T(8,128)}, bf16[12,64,512]{2,1,0:T(8,128)(2,1)}, f32[12,1,512]{2,1,0:T(1,128)}) custom-call(s32[14]{0:T(128)} %pad_add_fusion.info_ref, bf16[12,64,512]{2,1,0:T(8,128)(2,1)} %get-tuple-element.28.q_ref, bf16[27,1024,128]{2,1,0:T(8,128)(2,1)} %all-gather.2.cloned.1.call-done.kv_ref.hd_ref, ...), custom_call_target="tpu_custom_call" | custom-call | tf_op jit(solution)/shard_map/attend/pallas_call | solution.py:289
  149.7 3.3 convolution_convert_fusion
  153.0 0.6 all-reduce.11.cloned.1.call-start
  153.5 7.0 fusion.16
  160.5 24.2 %all-reduce.9.cloned.1.call-done = bf16[12,64,1024]{2,1,0:T(8,128)(2,1)} async-done(((bf16[12,64,1024]{2,1,0:T(8,128)(2,1)}), bf16[12,64,1024]{2,1,0:T(8,128)(2,1)}) %all-reduce.9.cloned.1.call-update) | async-done | bytes 1572880 | tf_op jit(solution)/shard_map/psum | solution.py:439
  184.7 2.6 multiply_reduce_fusion
  187.5 0.6 multiply_convert_fusion.3
  188.1 1.1 copy-done.27
  189.2 2.6 fusion.22
  191.9 5.2 multiply_convert_fusion.1
  197.1 2.6 fusion.20
  199.8 3.8 add_convert_fusion.1
  203.8 21.5 %all-reduce.11.cloned.1.call-done = bf16[12,64,1024]{2,1,0:T(8,128)(2,1)} async-done(((bf16[12,64,1024]{2,1,0:T(8,128)(2,1)}), bf16[12,64,1024]{2,1,0:T(8,128)(2,1)}) %all-reduce.11.cloned.1.call-update) | async-done | bytes 1572880 | tf_op jit(solution)/shard_map/psum | solution.py:439
  225.3 4.2 fusion.10
  229.5 2.8 fusion.36
  232.3 1.1 copy-done.15
  233.4 1.9 convolution_convert_fusion.1.do_ref
  235.3 27.5 %attend_back.1 = (f32[12,64,512]{2,1,0:T(8,128)}, bf16[24,1024,128]{2,1,0:T(8,128)(2,1)}, bf16[3,1024,128]{2,1,0:T(8,128)(2,1)}) custom-call(s32[14]{0:T(128)} %pad_add_fusion.info_ref, bf16[12,64,512]{2,1,0:T(8,128)(2,1)} %get-tuple-element.28.q_ref, bf16[27,1024,128]{2,1,0:T(8,128)(2,1)} %all-gather.2.cloned.1.call-done.kv_ref.hd_ref, ...), custom_call_target="tpu_custom_call" | custom-call | tf_op jit(solution)/shard_map/attend_back/pallas_call | solution.py:405
  262.8 6.5 pad_maximum_fusion
  269.7 6.2 fusion.28
  276.0 8.0 query_grads.1
  284.0 3.2 fusion.54
  287.2 2.7 fusion.42
  289.8 151.4 %reduce-scatter.2.cloned.1.call-done = bf16[27,64,128]{2,1,0:T(8,128)(2,1)} async-done(((bf16[27,1024,128]{2,1,0:T(8,128)(2,1)}), bf16[27,64,128]{2,1,0:T(8,128)(2,1)}) %reduce-scatter.2.cloned.1.call-update) | async-done | bytes 442384 | tf_op jit(solution)/shard_map/reduce_scatter | solution.py:533
  441.2 1.0 slice.94
  443.0 4.5 convolution_bitcast_fusion
  447.5 1.1 fusion.95
  448.6 0.6 fusion.47
  449.9 0.6 fusion.44
  450.4 0.7 copy-done.6
  451.2 1.0 copy-done.7
  452.3 2.2 add_convert_fusion
  454.8 6.3 bitcast_convert_fusion
  461.2 4.0 bitcast_convert_fusion.2
  465.2 4.0 bitcast_convert_fusion.1
  469.2 2.0 bitcast_convert_fusion.3
  471.2 1.2 fusion.33
  472.5 113.6 %all-reduce.13.cloned.1.call-done = f32[1024,640]{1,0:T(8,128)} async-done(((f32[1024,640]{1,0:T(8,128)}), f32[1024,640]{1,0:T(8,128)}) %all-reduce.13.cloned.1.call-update) | async-done | bytes 2621456 | tf_op jit(solution)/shard_map/psum | solution.py:561
  586.0 2.7 slice.101
  588.7 2.2 fusion.94
  590.9 20.2 %all-reduce.17.cloned.1.call-done = (bf16[12,64,1024]{2,1,0:T(8,128)(2,1)}, bf16[12,64,1024]{2,1,0:T(8,128)(2,1)}) async-done(((bf16[12,64,1024]{2,1,0:T(8,128)(2,1)}, bf16[12,64,1024]{2,1,0:T(8,128)(2,1)}), (bf16[12,64,1024]{2,1,0:T(8,128)(2,1)}, bf16[12,64,1024]{2,1,0:T(8,128)(2,1)})) %all-reduce.17.cloned.1.call-update) | async-done | bytes 3145744 | tf_op jit(solution)/shard_map/psum | solution.py:439
  611.1 2.8 fusion.15
  613.9 43.5 %all-reduce = (bf16[1024]{0:T(1024)(128)(2,1)S(1)}, bf16[1024]{0:T(1024)(128)(2,1)S(1)}) all-reduce(bf16[1024]{0:T(1024)(128)(2,1)S(1)} %get-tuple-element.44, bf16[1024]{0:T(1024)(128)(2,1)S(1)} %get-tuple-element.42), channel_id=1, replica_groups=mesh['seq'=16,'head'=2] {'seq'}, use_global_device_ids=true, to_apply=%region_10.11 | all-reduce | flops 2048 | bytes 8192 | tf_op jit(solution)/shard_map/psum | solution.py:556
  657.4 0.6 convert_element_type.154
  658.0 0.6 convert_element_type.160
  658.6 6.0 fusion.5
  664.6 250.7 %all-reduce.15.cloned.1.call-done = (bf16[1024,80]{0,1:T(8,128)(2,1)}, bf16[512,1024]{1,0:T(8,128)(2,1)}, bf16[1024,1408]{1,0:T(8,128)(2,1)}, bf16[1024,1408]{1,0:T(8,128)(2,1)}, bf16[1408,1024]{1,0:T(8,128)(2,1)}) async-done(((bf16[1024,80]{0,1:T(8,128)(2,1)}, bf16[512,1024]{1,0:T(8,128)(2,1)}, bf16[1024,1408]{1,0:T(8,128)(2,1)}, bf16[1024,1408]{1,0:T(8,128)(2,1)}, bf16[1408,1024]{1,0:T(8,128)(2,1)}), ...) | async-done | bytes 9863184 | tf_op jit(solution)/shard_map/psum | solution.py:556
  915.3 1.6 fusion.96
  916.9 1.6 slice.100
  918.5 2.8 convert_element_type.158
  921.3 2.9 convert_element_type.162
  924.3 2.9 convert_element_type.164
  927.3 3.2 convert_element_type.166
  (105 shorter events, 3.3 us)
Async XLA Ops:
  7.2 184.6 %copy-start = (bf16[1024,1408]{1,0:T(8,128)(2,1)S(1)}, bf16[1024,1408]{1,0:T(8,128)(2,1)}, u32[]{:S(2)}) copy-start(bf16[1024,1408]{1,0:T(8,128)(2,1)} %param.26) | copy-start | bytes 8650756
  7.2 125.3 %all-gather.2.cloned.1.call-start = ((), (), s32[]{:S(2)}) async-start(), calls=%async_computation.1 | async-start | bytes 7520256 | tf_op jit(solution)/shard_map/all_gather | solution.py:503
  15.9 11.1 %copy-start.26 = (s32[12]{0:T(128)S(1)}, s32[12]{0:T(128)}, u32[]{:S(2)}) copy-start(s32[12]{0:T(128)} %param.16) | copy-start | bytes 148
  27.0 157.7 %all-reduce.9.cloned.1.call-start = ((), (), s32[]{:S(2)}) async-start(), calls=%async_computation.2 | async-start | bytes 3145728 | tf_op jit(solution)/shard_map/psum | solution.py:439
  132.5 17.2 %copy-start.28 = (bf16[512,1024]{1,0:T(8,128)(2,1)S(1)}, bf16[512,1024]{1,0:T(8,128)(2,1)}, u32[]{:S(2)}) copy-start(bf16[512,1024]{1,0:T(8,128)(2,1)} %param.24) | copy-start | bytes 3145732
  153.0 72.3 %all-reduce.11.cloned.1.call-start = ((), (), s32[]{:S(2)}) async-start(), calls=%async_computation.3 | async-start | bytes 3145728 | tf_op jit(solution)/shard_map/psum | solution.py:439
  160.5 26.8 %copy-start.24 = (f32[1024]{0:T(1024)S(1)}, f32[1024]{0:T(1024)}, u32[]{:S(2)}) copy-start(f32[1024]{0:T(1024)} %param.25) | copy-start | bytes 12292
  184.7 2.6 copy-start.2
  184.7 2.8 copy-start.4
  187.3 1.9 copy-start.27
  187.5 4.3 slice-start
  189.2 2.6 copy-start.13
  189.2 2.6 slice-start.1
  197.1 2.6 copy-start.33
  197.1 2.6 copy-start.31
  203.5 25.9 %copy-start.3 = (bf16[12,64,1024]{2,1,0:T(8,128)(2,1)S(1)}, bf16[12,64,1024]{2,1,0:T(8,128)(2,1)}, u32[]{:S(2)}) copy-start(bf16[12,64,1024]{2,1,0:T(8,128)(2,1)} %x_ref.1) | copy-start | bytes 4718596
  203.5 237.7 %reduce-scatter.2.cloned.1.call-start = ((), (), s32[]{:S(2)}) async-start(), calls=%async_computation.4 | async-start | bytes 7520256 | tf_op jit(solution)/shard_map/reduce_scatter | solution.py:533
  225.3 4.2 copy-start.5
  229.5 4.0 copy-start.29
  232.3 1.1 copy-start.15
  269.3 316.7 %all-reduce.13.cloned.1.call-start = ((), (), s32[]{:S(2)}) async-start(), calls=%async_computation.5 | async-start | bytes 5242880 | tf_op jit(solution)/shard_map/psum | solution.py:561
  276.0 8.0 copy-start.21
  276.0 11.2 %copy-start.8 = (bf16[1024,384]{1,0:T(8,128)(2,1)S(1)}, bf16[1024,384]{1,0:T(8,128)(2,1)}, u32[]{:S(2)}) copy-start(bf16[1024,384]{1,0:T(8,128)(2,1)} %wqb_ref.1) | copy-start | bytes 2359300
  283.9 3.2 copy-start.20
  447.4 1.2 copy-start.22
  447.4 1.8 copy-start.23
  447.5 163.7 %all-reduce.17.cloned.1.call-start = ((), (), s32[]{:S(2)}) async-start(), calls=%async_computation.7 | async-start | bytes 6291456 | tf_op jit(solution)/shard_map/psum | solution.py:439
  448.6 1.2 copy-start.18
  449.3 1.9 copy-start.6
  449.3 2.9 copy-start.7
  449.3 3.0 copy-start.17
  454.5 460.8 %all-reduce.15.cloned.1.call-start = ((), (), s32[]{:S(2)}) async-start(), calls=%async_computation.6 | async-start | bytes 19726336 | tf_op jit(solution)/shard_map/psum | solution.py:556
  454.8 6.3 copy-start.14
  454.8 6.3 copy-start.32
  461.2 4.0 copy-start.34
  465.2 4.0 copy-start.16
  465.2 4.0 copy-start.30
  469.2 2.0 copy-start.12
  469.2 2.0 copy-start.19
  472.4 138.7 %copy-start.25 = (f32[1024]{0:T(1024)S(1)}, f32[1024]{0:T(1024)}, u32[]{:S(2)}) copy-start(f32[1024]{0:T(1024)} %param.17) | copy-start | bytes 12292
  915.3 6.0 copy-start.11
  921.3 3.0 copy-start.10
  924.3 3.0 copy-start.9
  927.2 3.3 copy-start.1
Sparse Core Ops, SparseCore 0:
  27.1 105.3 all-gather.1
  153.1 31.5 all-reduce.8
  203.7 21.5 all-reduce.10
  269.5 171.7 reduce-scatter.1
  447.6 138.4 all-reduce.12
  589.4 21.6 all-reduce.16
  619.8 295.4 all-reduce.14

commit v2 on v1

--- a/solution.py
+++ b/solution.py
@@ -415,6 +415,443 @@
     )(info, q, kv, kv, spread, o, do, lse)
 
 
+MESH = pl.DeviceIdType.MESH
+SIZES = {"z": 4, "y": 2, "x": 2}
+STRIDES = {"z": 4, "y": 2, "x": 1}
+CORES = 2
+
+
+def on_known_slice():
+    return lax.axis_size("seq") == math.prod(SIZES.values()) and lax.axis_size("head") == CORES
+
+
+class Links:
+    def __init__(self, send_sems, recv_sems):
+        self.seq = lax.axis_index("seq")
+        self.core = lax.axis_index("head")
+        self.at = {d: lax.rem(self.seq // STRIDES[d], SIZES[d]) for d in SIZES}
+        self.send_sems, self.recv_sems = send_sems, recv_sems
+        self.count = 0
+        self.started = []
+
+    def along(self, d, offset):
+        there = lax.rem(self.at[d] + offset, SIZES[d])
+        return there, (self.seq + (there - self.at[d]) * STRIDES[d], self.core)
+
+    def other_core(self):
+        return (self.seq, 1 - self.core)
+
+    def greet(self, core, chips=True):
+        barrier = pltpu.get_barrier_semaphore()
+        devices = [self.other_core()] if core else []
+        if chips:
+            devices += [self.along(d, o)[1] for d in SIZES for o in range(1, SIZES[d])]
+        for device in devices:
+            pl.semaphore_signal(barrier, inc=1, device_id=device, device_id_type=MESH)
+        pl.semaphore_wait(barrier, len(devices))
+
+    def send(self, src, dst, device):
+        copy = pltpu.make_async_remote_copy(
+            src_ref=src, dst_ref=dst, send_sem=self.send_sems.at[self.count], recv_sem=self.recv_sems.at[self.count],
+            device_id=device, device_id_type=MESH)
+        self.count += 1
+        copy.start()
+        self.started.append(copy)
+        return copy
+
+    def finish(self):
+        for copy in self.started:
+            copy.wait_send()
+
+
+def accumulate(acc, slots):
+    lead = acc.shape[:-2]
+
+    def body(i, carry):
+        at = []
+        for size in reversed(lead):
+            at.insert(0, lax.rem(i, size))
+            i = i // size
+        value = acc[(*at, slice(None), slice(None))].astype(F32)
+        for o in range(slots.shape[0]):
+            value = value + slots[(o, *at, slice(None), slice(None))].astype(F32)
+        acc[(*at, slice(None), slice(None))] = value.astype(BF16)
+        return carry
+
+    lax.fori_loop(0, math.prod(lead), body, 0)
+
+
+def scatter_steps(links, order, source, acc, slots, ready):
+    fixed = {}
+    for k, d in enumerate(order):
+        copies = []
+        for o in range(1, SIZES[d]):
+            there, device = links.along(d, o)
+            view = source if k == 0 else acc
+            copies.append(links.send(view({**fixed, d: there}), slots[k].at[o - 1], device))
+        yield
+        if k == 0:
+            ready()
+        for copy in copies:
+            copy.wait_recv()
+        fixed[d] = links.at[d]
+        accumulate(acc(fixed), slots[k])
+
+
+def gather_steps(links, order, out, first):
+    for k in reversed(range(len(order))):
+        fixed = {d: links.at[d] for d in order[: k + 1]}
+        copies = []
+        for o in range(1, SIZES[order[k]]):
+            _, device = links.along(order[k], o)
+            src = first if first is not None and k == len(order) - 1 else out(fixed)
+            copies.append(links.send(src, out(fixed), device))
+        yield
+        for copy in copies:
+            copy.wait_recv()
+
+
+def run_waves(groups):
+    live, waiting = [], list(groups)
+    while live or waiting:
+        if waiting:
+            live.append(list(waiting.pop(0)))
+        for group in live:
+            group[:] = [job for job in group if next(job, "end") != "end"]
+        live = [group for group in live if group]
+
+
+def slot_shapes(order, units, tail):
+    shapes, open_dims = [], list(SIZES)
+    for d in order:
+        open_dims.remove(d)
+        shapes.append((SIZES[d] - 1, *units, *[SIZES[e] for e in open_dims], *tail))
+    return shapes
+
+
+def pick(ref, lead, sel, axes, tail=()):
+    return ref.at[(*lead, *[sel.get(d, slice(None)) for d in axes], *tail)]
+
+
+ZYX = ("z", "y", "x")
+
+
+def collect_jobs(rows, packs):
+    step = 4
+    own = [(rows + u, min(step, rows - u)) for u in range(0, rows, step)]
+    jobs = own + [(2 * rows, packs)]
+    half = (len(jobs) + 1) // 2
+    return [(first, n, ("y", "x", "z") if i < half else ("x", "y", "z")) for i, (first, n) in enumerate(jobs)]
+
+
+def collect_kernel(rows, packs, kv_ref, hd_ref, out_ref, local_sems, send_sems, recv_sems):
+    links = Links(send_sems, recv_sems)
+    links.greet(core=True)
+    own = tuple(links.at[d] for d in ZYX)
+    locals_ = []
+    jobs = collect_jobs(rows, packs)
+    for i, (first, n, _) in enumerate(jobs):
+        src = hd_ref if first == 2 * rows else kv_ref.at[pl.ds(links.core * rows + first - rows, n)]
+        copy = pltpu.make_async_copy(src, out_ref.at[(pl.ds(first, n), *own)], local_sems.at[i])
+        copy.start()
+        locals_.append(copy)
+
+    def job(i, first, n, order):
+        locals_[i].wait()
+        yield from gather_steps(links, order, lambda sel: pick(out_ref, [pl.ds(first, n)], sel, ZYX), None)
+        if first < 2 * rows:
+            copy = links.send(out_ref.at[pl.ds(first, n)], out_ref.at[pl.ds(first - rows, n)], links.other_core())
+            yield
+            copy.wait_recv()
+
+    made = [job(i, *j) for i, j in enumerate(jobs)]
+    half = (len(made) + 1) // 2
+    run_waves(list(zip(made[:half], made[half:])))
+    links.finish()
+
+
+def collect(kv, hd):
+    units, tokens, _ = kv.shape
+    packs = hd.shape[0]
+    rows = units // 2
+    copies = 8 * len(collect_jobs(rows, packs))
+    out = pl.pallas_call(
+        functools.partial(collect_kernel, rows, packs),
+        out_shape=jax.ShapeDtypeStruct((units + packs, *[SIZES[d] for d in ZYX], tokens, LANES), BF16),
+        in_specs=[pl.BlockSpec(memory_space=pl.ANY)] * 2,
+        out_specs=pl.BlockSpec(memory_space=pl.ANY),
+        scratch_shapes=[pltpu.SemaphoreType.DMA((8,)), pltpu.SemaphoreType.DMA((copies,)), pltpu.SemaphoreType.DMA((copies,))],
+        compiler_params=pltpu.CompilerParams(collective_id=1, has_side_effects=True),
+        name="collect",
+    )(kv, hd)
+    return out.reshape(units + packs, -1, LANES)
+
+
+def return_kernel(rows, packs, dkv_ref, dhd_ref, out_ref, acc_ref, core_ref, *rest):
+    jobs = collect_jobs(rows, packs)
+    slot_refs, (local_sems, send_sems, recv_sems) = rest[: 3 * len(jobs)], rest[3 * len(jobs) :]
+    links = Links(send_sems, recv_sems)
+    links.greet(core=True)
+    own = tuple(links.at[d] for d in ZYX)
+    loads, swaps = [], []
+    for i, (first, n, _) in enumerate(jobs):
+        heads = first == 2 * rows
+        part = pl.ds(first - rows, n)
+        if not heads:
+            swaps.append(links.send(dkv_ref.at[part], core_ref.at[part], links.other_core()))
+        load = pltpu.make_async_copy(dhd_ref if heads else dkv_ref.at[pl.ds(first, n)], acc_ref.at[part], local_sems.at[i])
+        load.start()
+        loads.append(load)
+    out_ref[...] = jnp.zeros_like(out_ref)
+
+    def job(i, first, n, order):
+        heads = first == 2 * rows
+        part = pl.ds(first - rows, n)
+        loads[i].wait()
+        if not heads:
+            swaps[i].wait_recv()
+
+            def add(j, carry):
+                u = first - rows + j // SIZES["z"]
+                z = lax.rem(j, SIZES["z"])
+                acc_ref[u, z] = (acc_ref[u, z].astype(F32) + core_ref[u, z].astype(F32)).astype(BF16)
+                return carry
+
+            lax.fori_loop(0, n * SIZES["z"], add, 0)
+
+        def view(sel):
+            return pick(acc_ref, [part], sel, ZYX)
+
+        yield from scatter_steps(links, order, view, view, slot_refs[3 * i : 3 * i + 3], lambda: None)
+        for u in range(n):
+            at = 2 * rows + u if heads else links.core * rows + first - rows + u
+            out_ref[at] = acc_ref[(first - rows + u, *own)]
+
+    made = [job(i, *j) for i, j in enumerate(jobs)]
+    half = (len(made) + 1) // 2
+    run_waves(list(zip(made[:half], made[half:])))
+    links.finish()
+
+
+def give_back(dkv, dhd):
+    units, length, _ = dkv.shape
+    packs = dhd.shape[0]
+    rows = units // 2
+    tokens = length // math.prod(SIZES.values())
+    dims = tuple(SIZES[d] for d in ZYX)
+    jobs = collect_jobs(rows, packs)
+    slots = [pltpu.VMEM(shape, BF16) for _, n, order in jobs for shape in slot_shapes(order, (n,), (tokens, LANES))]
+    copies = 8 * len(jobs)
+    return pl.pallas_call(
+        functools.partial(return_kernel, rows, packs),
+        out_shape=jax.ShapeDtypeStruct((units + packs, tokens, LANES), BF16),
+        in_specs=[pl.BlockSpec(memory_space=pl.ANY)] * 2,
+        out_specs=pl.BlockSpec(memory_space=pltpu.VMEM),
+        scratch_shapes=[pltpu.VMEM((rows + packs, *dims, tokens, LANES), BF16), pltpu.VMEM((rows, *dims, tokens, LANES), BF16),
+                        *slots, pltpu.SemaphoreType.DMA((8,)), pltpu.SemaphoreType.DMA((copies,)), pltpu.SemaphoreType.DMA((copies,))],
+        compiler_params=pltpu.CompilerParams(collective_id=2, has_side_effects=True, vmem_limit_bytes=48 * 2**20),
+        name="give_back",
+    )(dkv.reshape(units, *dims, tokens, LANES), dhd.reshape(packs, *dims, tokens, LANES))
+
+
+def pair_kernel(x_ref, out_ref, got_ref, send_sems, recv_sems):
+    links = Links(send_sems, recv_sems)
+    links.greet(core=True, chips=False)
+    copies = [links.send(x_ref.at[r], got_ref.at[r], links.other_core()) for r in range(x_ref.shape[0])]
+    for r, copy in enumerate(copies):
+        copy.wait_recv()
+        out_ref[r] = (x_ref[r].astype(F32) + got_ref[r].astype(F32)).astype(out_ref.dtype)
+    links.finish()
+
+
+def pair_sum(x, ident):
+    parts = 4
+    rows, tokens, model = x.shape
+    flat = x.reshape(parts, rows * tokens // parts, model)
+    return pl.pallas_call(
+        pair_kernel,
+        out_shape=jax.ShapeDtypeStruct(flat.shape, BF16),
+        in_specs=[pl.BlockSpec(memory_space=pltpu.VMEM)],
+        out_specs=pl.BlockSpec(memory_space=pltpu.VMEM),
+        scratch_shapes=[pltpu.VMEM(flat.shape, BF16), pltpu.SemaphoreType.DMA((parts,)), pltpu.SemaphoreType.DMA((parts,))],
+        compiler_params=pltpu.CompilerParams(collective_id=ident, has_side_effects=True, vmem_limit_bytes=32 * 2**20),
+        name="pair_sum_%d" % ident,
+    )(flat).reshape(x.shape)
+
+
+class Cut:
+    def __init__(self, array, axes, rows, cols, order, lane_dim=None, shared=False):
+        self.array, self.axes, self.rows, self.cols = array, axes, rows, cols
+        self.order, self.lane_dim, self.shared = order, lane_dim, shared
+
+    def tail(self):
+        return (self.rows[1], self.cols[1])
+
+    def view(self, ref, sel, core):
+        cols = pl.ds(self.cols[0], self.cols[1])
+        if self.lane_dim is not None:
+            cols = pl.ds(pl.multiple_of(self.cols[0] + sel[self.lane_dim] * self.cols[1], LANES), self.cols[1])
+        lead = [core] if self.shared else []
+        return pick(ref, lead, sel, self.axes, (pl.ds(self.rows[0], self.rows[1]), cols))
+
+    def inner(self):
+        return tuple(d for d in self.axes if d != self.order[0])
+
+    def acc_shape(self):
+        return (*[SIZES[d] for d in self.inner()], *self.tail())
+
+    def slots(self):
+        shapes, open_dims = [], list(self.inner())
+        for d in self.order:
+            if d in open_dims:
+                open_dims.remove(d)
+            shapes.append((SIZES[d] - 1, *[SIZES[e] for e in open_dims], *self.tail()))
+        return shapes
+
+
+def weight_cuts(shapes):
+    a, b, c, d = ("x", "y", "z"), ("y", "x", "z"), ("x", "z", "y"), ("y", "z", "x")
+    groups = []
+    gate_rows, gate_cols = shapes[0][3:]
+    parts = 2
+    for i in range(parts):
+        rows = (i * gate_rows // parts, gate_rows // parts)
+        groups.append([Cut(0, ("x", "y", "z"), rows, (0, gate_cols), a), Cut(1, ("x", "y", "z"), rows, (0, gate_cols), b)])
+    down_rows, down_cols = shapes[2][2:]
+    groups.append([Cut(2, ("y", "z"), (0, down_rows), (0, down_cols // 4), c, lane_dim="x"),
+                   Cut(2, ("x", "z"), (0, down_rows), (down_cols // 2, down_cols // 4), d, lane_dim="y")])
+    out_rows, out_cols = shapes[3][3:]
+    basis_rows, basis_cols = shapes[4][4:]
+    head_rows, head_cols = shapes[5][3:]
+    axes = ("x", "y", "z")
+    cut = basis_cols // LANES // 2 * LANES
+    groups.append([Cut(3, axes, (0, out_rows), (0, out_cols // 2), a),
+                   Cut(3, axes, (0, out_rows), (out_cols // 2, out_cols // 2), b),
+                   Cut(4, axes, (0, basis_rows), (0, cut), a, shared=True),
+                   Cut(4, axes, (0, basis_rows), (cut, basis_cols - cut), b, shared=True),
+                   Cut(5, axes, (0, head_rows), (0, head_cols), a)])
+    return groups
+
+
+def weight_kernel(groups, count, *refs):
+    jobs = [cut for group in groups for cut in group]
+    ins, outs = refs[:count], refs[count : 2 * count]
+    at = 2 * count
+    accs = refs[at : at + len(jobs)]
+    at += len(jobs)
+    slots = refs[at : at + 3 * len(jobs)]
+    at += 3 * len(jobs)
+    shared_own, shared_got, local_sems, send_sems, recv_sems = refs[at:]
+    links = Links(send_sems, recv_sems)
+    links.greet(core=True)
+    loads = []
+    for i, cut in enumerate(jobs):
+        if cut.shared:
+            loads.append(None)
+            continue
+        load = pltpu.make_async_copy(cut.view(ins[cut.array], {cut.order[0]: links.at[cut.order[0]]}, links.core), accs[i],
+                                     local_sems.at[i])
+        load.start()
+        loads.append(load)
+    basis = next(cut.array for cut in jobs if cut.shared)
+    own = pltpu.make_async_copy(ins[basis].at[links.core], shared_own, local_sems.at[len(jobs)])
+    own.start()
+    swap = links.send(ins[basis].at[1 - links.core], shared_got, links.other_core())
+    stores = []
+
+    def job(i, cut):
+        def acc(sel):
+            return pick(accs[i], [], sel, cut.inner())
+
+        def source(sel):
+            return cut.view(ins[cut.array], sel, links.core)
+
+        ready = loads[i].wait if loads[i] is not None else lambda: None
+        if cut.shared:
+            summed = pick(shared_own, [], {cut.order[0]: links.at[cut.order[0]]}, cut.axes,
+                          (slice(None), pl.ds(cut.cols[0], cut.cols[1])))
+
+            def keep(j, carry):
+                p, q = j // accs[i].shape[1], lax.rem(j, accs[i].shape[1])
+                accs[i][p, q] = summed[p, q]
+                return carry
+
+            lax.fori_loop(0, accs[i].shape[0] * accs[i].shape[1], keep, 0)
+
+            def source(sel):
+                return pick(shared_own, [], sel, cut.axes, (slice(None), pl.ds(cut.cols[0], cut.cols[1])))
+
+        yield from scatter_steps(links, cut.order, source, acc, slots[3 * i : 3 * i + 3], ready)
+        piece = acc({d: links.at[d] for d in cut.inner()})
+
+        def out(sel):
+            return cut.view(outs[cut.array], sel, links.core)
+
+        store = pltpu.make_async_copy(piece, out(links.at), local_sems.at[len(jobs) + 1 + i])
+        store.start()
+        steps = gather_steps(links, cut.order, out, piece)
+        next(steps)
+        yield
+        store.wait()
+        yield from steps
+
+    def first_shared():
+        own.wait()
+        swap.wait_recv()
+
+        def add(j, carry):
+            shape = shared_own.shape
+            p, q, r = j // (shape[1] * shape[2]), lax.rem(j // shape[2], shape[1]), lax.rem(j, shape[2])
+            shared_own[p, q, r] = (shared_own[p, q, r].astype(F32) + shared_got[p, q, r].astype(F32)).astype(BF16)
+            return carry
+
+        lax.fori_loop(0, math.prod(shared_own.shape[:3]), add, 0)
+        return
+        yield
+
+    made, i = [], 0
+    for group in groups:
+        lot = []
+        if any(cut.shared for cut in group):
+            lot.append(first_shared())
+        for cut in group:
+            lot.append(job(i, cut))
+            i += 1
+        made.append(lot)
+    run_waves(made)
+    last = links.send(outs[basis].at[links.core], outs[basis].at[links.core], links.other_core())
+    last.wait_recv()
+    links.finish()
+
+
+def weight_sums(gate, up, down, out_proj, basis, heads):
+    dims = tuple(SIZES[d] for d in ("x", "y", "z"))
+
+    def pieces(w):
+        return w.reshape(*dims, w.shape[0] // math.prod(dims), w.shape[1])
+
+    half = basis.reshape(CORES, *dims, basis.shape[0] // CORES // math.prod(dims), basis.shape[1])
+    arrays = [pieces(gate), pieces(up), down.reshape(2, SIZES["z"], -1, down.shape[1]), pieces(out_proj), half, pieces(heads)]
+    groups = weight_cuts([w.shape for w in arrays])
+    jobs = [cut for group in groups for cut in group]
+    accs = [pltpu.VMEM(cut.acc_shape(), BF16) for cut in jobs]
+    slots = [pltpu.VMEM(shape, BF16) for cut in jobs for shape in cut.slots()]
+    copies = 10 * len(jobs) + 4
+    any_space = pl.BlockSpec(memory_space=pl.ANY)
+    outs = pl.pallas_call(
+        functools.partial(weight_kernel, groups, len(arrays)),
+        out_shape=[jax.ShapeDtypeStruct(w.shape, BF16) for w in arrays],
+        in_specs=[any_space] * len(arrays),
+        out_specs=[any_space] * len(arrays),
+        scratch_shapes=[*accs, *slots, pltpu.VMEM(half.shape[1:], BF16), pltpu.VMEM(half.shape[1:], BF16),
+                        pltpu.SemaphoreType.DMA((2 * len(jobs) + 1,)), pltpu.SemaphoreType.DMA((copies,)),
+                        pltpu.SemaphoreType.DMA((copies,))],
+        compiler_params=pltpu.CompilerParams(collective_id=3, has_side_effects=True, vmem_limit_bytes=48 * 2**20),
+        name="weight_sums",
+    )(*arrays)
+    return [o.reshape(w.shape) for o, w in zip(outs, (gate, up, down, out_proj, basis, heads))]
+
+
 def norm_back(inputs, row_scale, gain_vec, grad_rows):
     weighted = grad_rows * gain_vec
     cubed = row_scale * row_scale * row_scale
@@ -435,7 +872,9 @@
     return jnp.einsum("rsd,rse->de", normed, grad_rows, preferred_element_type=F32)
 
 
-def head_sum(partial):
+def head_sum(partial, ident):
+    if on_known_slice():
+        return pair_sum(partial.astype(BF16), ident).astype(F32)
     return lax.psum(partial.astype(BF16), "head").astype(F32)
 
 
@@ -500,11 +939,15 @@
         pack_rows, width)
     inputs = block_input.astype(F32)
     scale_one = rms_scale(inputs)
-    kv = lax.all_gather(jnp.concatenate([own_kv, own_heads], axis=0), "seq", axis=1, tiled=True)
-    shift = jnp.zeros((), jnp.int32)
+    if on_known_slice():
+        kv = collect(own_kv, own_heads)
+        shift = (1 - lax.axis_index("head")) * (row_count // CORES)
+    else:
+        kv = lax.all_gather(jnp.concatenate([own_kv, own_heads], axis=0), "seq", axis=1, tiled=True)
+        shift = jnp.zeros((), jnp.int32)
     info = jnp.stack([*[seq_lengths[r] for r in range(row_count)], shift, first_slot]).astype(jnp.int32)
     attended, mixed_flat, lse = attend(info, queries, kv, shift, spread, pack_rows, group, block)
-    attn_out = head_sum(project(mixed_flat, out_project))
+    attn_out = head_sum(project(mixed_flat, out_project), 4)
     middle = inputs + attn_out
     scale_two = rms_scale(middle)
     normed_two = (middle * scale_two * ffn_gain).astype(BF16)
@@ -513,7 +956,7 @@
     sigmoid_gate = jax.nn.sigmoid(gate_act)
     silu_gate = gate_act * sigmoid_gate
     hidden = (silu_gate * up_act).astype(BF16)
-    ffn_out = head_sum(project(hidden, down_weight))
+    ffn_out = head_sum(project(hidden, down_weight), 5)
     block_output = (middle + ffn_out).astype(BF16)
     cotangent = out_cotangent.astype(F32)
     down_grad = jnp.einsum("rsf,rsd->fd", hidden, out_cotangent, preferred_element_type=F32)
@@ -522,7 +965,7 @@
     d_up = (d_hidden * silu_gate).astype(BF16)
     gate_grad = weight_grad(normed_two, d_gate)
     up_grad = weight_grad(normed_two, d_up)
-    d_normed_two = head_sum(back_project(d_gate, gate_weight) + back_project(d_up, up_weight))
+    d_normed_two = head_sum(back_project(d_gate, gate_weight) + back_project(d_up, up_weight), 6)
     d_middle_norm, ffn_gain_part = norm_back(middle, scale_two, ffn_gain, d_normed_two)
     d_middle = cotangent + d_middle_norm
     d_branch = d_middle.astype(BF16)
@@ -530,8 +973,11 @@
     d_mixed = back_project(d_branch, out_project).astype(BF16)
     d_queries, d_kv, d_heads = attend_back(info, queries, kv, spread, attended, d_mixed, lse, pack_rows, group, block)
     dq_heads, dq_basis = query_grads(d_queries, aq, bq, query_spread, cos, sin, pack_rows)
-    key_grads = lax.psum_scatter(
-        jnp.concatenate([d_kv, d_heads], axis=0), "seq", scatter_dimension=1, tiled=True)
+    if on_known_slice():
+        key_grads = give_back(d_kv, d_heads)
+    else:
+        key_grads = lax.psum_scatter(
+            jnp.concatenate([d_kv, d_heads], axis=0), "seq", scatter_dimension=1, tiled=True)
     d_kv_own = key_grads[: 2 * row_count].reshape(row_count, 2, slot_count, LANES).astype(F32)
     half = DH // 2
     pairs = d_kv_own[:, 0].reshape(row_count, slot_count, 2, 2, half)
@@ -546,19 +992,25 @@
     d_normed = head_sum(
         back_project(dq_heads, query_heads) + back_project(dq_basis, query_basis)
         + back_project(dk_heads, key_heads) + back_project(dk_basis, key_basis)
-        + back_project(dv_heads, value_heads) + back_project(dv_basis, value_basis))
+        + back_project(dv_heads, value_heads) + back_project(dv_basis, value_basis), 7)
     d_input_norm, attn_gain_part = norm_back(inputs, scale_one, attn_gain, d_normed)
     input_grad = d_middle + d_input_norm
     head_grads = weight_grad(normed, jnp.concatenate([dq_heads, dk_heads, dv_heads], axis=-1))
     basis_grads = weight_grad(normed, jnp.concatenate([dq_basis, dk_basis, dv_basis], axis=-1))
 
-    def seq_sum(*parts):
-        return tuple(t.astype(F32) for t in lax.psum(tuple(t.astype(BF16) for t in parts), "seq"))
-
-    gate_grad, up_grad, down_grad = seq_sum(gate_grad, up_grad, down_grad)
-    out_project_grad, head_grads, attn_gain_part, ffn_gain_part = seq_sum(
-        out_project_grad, head_grads, attn_gain_part, ffn_gain_part)
-    basis_grads = lax.psum(basis_grads, ("seq", "head"))
+    gains = jnp.stack([attn_gain_part, ffn_gain_part], axis=1)
+    small = jnp.concatenate([head_grads, gains], axis=1)
+    if on_known_slice():
+        small = jnp.pad(small, ((0, 0), (0, -small.shape[1] % LANES)))
+        sums = weight_sums(*[t.astype(BF16) for t in (gate_grad, up_grad, down_grad, out_project_grad, basis_grads, small)])
+        gate_grad, up_grad, down_grad, out_project_grad, basis_grads, small = [t.astype(F32) for t in sums]
+    else:
+        sums = lax.psum(tuple(t.astype(BF16) for t in (gate_grad, up_grad, down_grad, out_project_grad, small)), "seq")
+        gate_grad, up_grad, down_grad, out_project_grad, small = [t.astype(F32) for t in sums]
+        basis_grads = lax.psum(basis_grads, ("seq", "head"))
+    head_grads = small
+    gain_at = head_count * (RQ + RK + RV)
+    attn_gain_part, ffn_gain_part = small[:, gain_at], small[:, gain_at + 1]
     nq, nk = head_count * RQ, head_count * RK
     return (
         block_output,
@@ -568,7 +1020,7 @@
         basis_grads[:, : RQ * DH],
         head_grads[:, nq : nq + nk],
         basis_grads[:, RQ * DH : (RQ + RK) * DH],
-        head_grads[:, nq + nk :],
+        head_grads[:, nq + nk : gain_at],
         basis_grads[:, (RQ + RK) * DH :],
         out_project_grad,
         ffn_gain_part,

time: 949 us -> 545 us (0.57)
  the two profiles are of different devices: /device:TPU:0 before, /device:TPU:29 now
where the time goes in v2:
time: 545 us; the launch traced here: 535 us
  Pallas kernels  440 us (81%)
  matrix products  44.6 us (8%)
  other arithmetic  28.2 us (5%)
  local copies, waits for them, and re-layouts  20.4 us (4%)
    pallas_call x1, Pallas kernels, weight_sums(): pl.pallas_call(functools.partial(weight_kernel, groups, len(arrays)), out...  219 us
    pallas_call x1, Pallas kernels, collect(): pl.pallas_call(functools.partial(collect_kernel, rows, packs), out_shape=...  58.8 us
    pallas_call x1, Pallas kernels, give_back(): pl.pallas_call(functools.partial(return_kernel, rows, packs), out_shape=j...  55.4 us
    pallas_call x1, Pallas kernels, attend_back(): pl.pallas_call(functools.partial(attend_back_kernel, pack_rows, group, bl...  45 us
    pallas_call x1, Pallas kernels, attend(): pl.pallas_call(functools.partial(attend_kernel, pack_rows, group, block),...  28.4 us
    pallas_call x4, Pallas kernels, pair_sum(): pl.pallas_call(pair_kernel, out_shape=jax.ShapeDtypeStruct(flat.shape, BF...  17.3 us
    dot_general x4, matrix products, project(): jnp.einsum('rsd,de->rse', activations, weight, preferred_element_type=F32)  15.4 us
    convert_element_type x6, other arithmetic, shards(): t.astype(F32)  13.4 us

profile of v2, /device:TPU:29, one launch (start us, length us, event | category | flops | bytes accessed | tf_op | source)
XLA Modules:
  0.0 535.4 jit_solution(1312225366535207470)
XLA Ops:
  0.9 0.7 pad_maximum_fusion.3
  1.7 0.8 select_convert_fusion.1.eq_ref
  2.4 0.9 copy.123
  3.4 0.9 copy.124
  4.3 3.9 concatenate.25.wh_ref
  8.2 0.8 copy.132.wqh_ref
  9.1 8.5 %factors.1 = (bf16[12,64,1024]{2,1,0:T(8,128)(2,1)}, f32[12,64,48]{2,1,0:T(8,128)}, f32[12,64,384]{2,1,0:T(8,128)}, bf16[12,64,512]{2,1,0:T(8,128)(2,1)}, bf16[2...) custom-call(bf16[12,64,1024]{2,1,0:T(8,128)(2,1)} %x_ref.1, f32[1,1024]{1,0:T(1,128)} %bitcast.170, ...), custom_call_target="tpu_custom_call" | custom-call | tf_op jit(solution)/shard_map/factors/pallas_call | solution.py:119
  17.6 58.8 %collect.1 = bf16[27,4,2,2,64,128]{5,4,3,2,1,0:T(8,128)(2,1)} custom-call(bf16[24,64,128]{2,1,0:T(8,128)(2,1)} %get-tuple-element.35.kv_ref, bf16[3,64,128]{2,1,0:T(8,128)(2,1)} %get-tuple-element.36.hd_ref), custom_call_target="tpu_custom_call" | custom-call | tf_op jit(solution)/shard_map/collect/pallas_call | solution.py:578
  76.3 0.6 pad_add_fusion.info_ref
  77.1 1.9 select_convert_fusion.spread_ref
  78.9 28.4 %attend.1 = (f32[12,64,512]{2,1,0:T(8,128)}, bf16[12,64,512]{2,1,0:T(8,128)(2,1)}, f32[12,1,512]{2,1,0:T(1,128)}) custom-call(s32[14]{0:T(128)} %pad_add_fusion.info_ref, bf16[12,64,512]{2,1,0:T(8,128)(2,1)} %get-tuple-element.34.q_ref, bf16[27,1024,128]{2,1,0:T(8,128)(2,1)} %bitcast.153, bf16[27,1024,128]{2,1,0:T(8,128)(2,1)} %bitcast.154, ...), custom_call_target="tpu_custom_call" | custom-call | tf_op jit(solution)/shard_map/attend/pallas_call | solution.py:289
  107.4 2.2 convolution_convert_fusion
  109.6 3.6 pair_sum_4.1
  113.2 0.6 multiply_reduce_fusion
  113.9 0.6 multiply_convert_fusion.3
  114.4 1.2 copy-done.42
  115.7 2.6 fusion.23
  118.5 2.6 fusion.17
  121.2 5.4 %multiply_convert_fusion.1 = (bf16[12,64,1408]{2,1,0:T(8,128)(2,1)S(1)}, bf16[12,64,1408]{2,1,0:T(8,128)(2,1)S(1)}, bf16[12,64,1408]{2,1,0:T(8,128)(2,1)}) fusion(f32[12,64,1408]{2,1,0:T(8,128)S(1)} %fusion.17, f32[12,64,1408]{2,1,0:T(8,128)S(1)} %fusion.23, bf16[12,64,1024]{2,1,0:T(8,128)(2,1)S(1)} %multiply_convert_fusion.3, bf16[1024,1408]{1,0:T(8,128)(2,1)S(1)} %copy-done), kind=kOutput, calls=%fused_computation.9 | convolution fusion | flops 2230812672 | bytes 19595264 | tf_op jit(solution)/shard_map/rsd,de->rse/dot_general | solution.py:864
  126.6 2.6 fusion.21
  129.2 2.6 add_convert_fusion.1
  131.8 3.6 pair_sum_6.1
  135.5 2.3 fusion.10
  137.8 1.3 fusion.37
  139.1 2.0 convolution_convert_fusion.1.do_ref
  141.1 45.0 %attend_back.1 = (f32[12,64,512]{2,1,0:T(8,128)}, bf16[24,1024,128]{2,1,0:T(8,128)(2,1)}, bf16[3,1024,128]{2,1,0:T(8,128)(2,1)}) custom-call(s32[14]{0:T(128)} %pad_add_fusion.info_ref, bf16[12,64,512]{2,1,0:T(8,128)(2,1)} %get-tuple-element.34.q_ref, bf16[27,1024,128]{2,1,0:T(8,128)(2,1)} %bitcast.155, bf16[27,1024,128]{2,1,0:T(8,128)(2,1)} %bitcast.156, ...), custom_call_target="tpu_custom_call" | custom-call | tf_op jit(solution)/shard_map/attend_back/pallas_call | solution.py:405
  186.0 8.3 %query_grads.1 = (bf16[12,64,48]{2,1,0:T(8,128)(2,1)}, bf16[12,64,384]{2,1,0:T(8,128)(2,1)}) custom-call(f32[12,64,512]{2,1,0:T(8,128)} %get-tuple-element.40.dq_ref, f32[12,64,48]{2,1,0:T(8,128)} %get-tuple-element.41.aq_ref, f32[12,64,384]{2,1,0:T(8,128)} %get-tuple-element.42.bq_ref, bf16[48,3072]{1,0:T(8,128)(2,1)} %select_convert_fusion.1.eq_ref, ...), custom_call_target="tpu_custom_call" | custom-call | tf_op jit(solution)/shard_map/query_grads/pallas_call | solution.py:180
  194.4 55.4 %give_back.1 = bf16[27,64,128]{2,1,0:T(8,128)(2,1)S(1)} custom-call(bf16[24,4,2,2,64,128]{5,4,3,2,1,0:T(8,128)(2,1)} %bitcast.158, bf16[3,4,2,2,64,128]{5,4,3,2,1,0:T(8,128)(2,1)S(1)} %bitcast.152), custom_call_target="tpu_custom_call" | custom-call | tf_op jit(solution)/shard_map/give_back/pallas_call | solution.py:645
  250.0 0.5 fusion.34
  250.5 0.7 slice_bitcast_fusion
  251.6 0.8 copy.136
  252.7 1.0 fusion.43
  253.8 0.5 fusion.55
  254.3 0.6 fusion.48
  255.0 0.5 fusion.50
  255.5 0.6 fusion.45
  256.1 0.9 add_convert_fusion
  257.1 6.6 %pair_sum_7.1 = bf16[4,192,1024]{2,1,0:T(8,128)(2,1)S(1)} custom-call(bf16[4,192,1024]{2,1,0:T(8,128)(2,1)S(1)} %bitcast.144), custom_call_target="tpu_custom_call" | custom-call | tf_op jit(solution)/shard_map/pair_sum_7/pallas_call | solution.py:671
  263.7 1.1 copy-done.6
  264.8 1.4 fusion.15
  266.7 1.4 bitcast_convert_fusion.6
  268.2 0.6 copy-done.47
  268.8 4.0 bitcast_convert_fusion.2
  272.8 4.2 bitcast_convert_fusion.1
  277.0 1.0 bitcast_convert_fusion.7
  278.0 0.4 copy-done.13
  278.4 0.7 copy-done.50
  279.0 4.0 bitcast_convert_fusion
  283.1 218.8 %weight_sums.1 = (bf16[2,2,4,64,1408]{4,3,2,1,0:T(8,128)(2,1)}, bf16[2,2,4,64,1408]{4,3,2,1,0:T(8,128)(2,1)}, bf16[2,4,176,1024]{3,2,1,0:T(8,128)(2,1)}, bf16[2,...) custom-call(bf16[2,2,4,64,1408]{4,3,2,1,0:T(8,128)(2,1)} %bitcast.16, ...), custom_call_target="tpu_custom_call" | custom-call | tf_op jit(solution)/shard_map/weight_sums/pallas_call | solution.py:841
  501.9 5.2 bitcast_convert_fusion.3
  507.1 3.1 bitcast_convert_fusion.4
  510.2 3.1 bitcast_convert_fusion.5
  513.6 1.2 slice.105
  514.9 1.0 fusion.95
  515.9 1.6 bitcast_convert_fusion.9
  517.6 0.3 fusion.97
  517.9 0.8 copy.156
  518.7 0.8 copy.157
  519.9 0.8 copy.154
  520.6 0.8 copy.158
  521.4 0.9 copy.155
  522.3 5.2 fusion.29
  527.5 3.6 pair_sum_5.1
  531.2 4.0 fusion.8
  (126 shorter events, 2.7 us)
Async XLA Ops:
  0.6 120.5 %copy-start = (bf16[1024,1408]{1,0:T(8,128)(2,1)S(1)}, bf16[1024,1408]{1,0:T(8,128)(2,1)}, u32[]{:S(2)}) copy-start(bf16[1024,1408]{1,0:T(8,128)(2,1)} %param.26) | copy-start | bytes 8650756
  0.7 7.6 %copy-start.28 = (bf16[1024,48]{0,1:T(8,128)(2,1)S(1)}, bf16[1024,48]{0,1:T(8,128)(2,1)}, u32[]{:S(2)}) copy-start(bf16[1024,48]{0,1:T(8,128)(2,1)} %param.18) | copy-start | bytes 294916
  0.9 0.8 copy-start.30
  17.5 58.8 %copy-start.41 = (s32[12]{0:T(128)S(1)}, s32[12]{0:T(128)}, u32[]{:S(2)}) copy-start(s32[12]{0:T(128)} %param.16) | copy-start | bytes 148
  78.9 28.4 %copy-start.44 = (bf16[512,1024]{1,0:T(8,128)(2,1)S(1)}, bf16[512,1024]{1,0:T(8,128)(2,1)}, u32[]{:S(2)}) copy-start(bf16[512,1024]{1,0:T(8,128)(2,1)} %param.24) | copy-start | bytes 3145732
  107.4 5.9 %copy-start.9 = (bf16[12,64,1024]{2,1,0:T(8,128)(2,1)S(1)}, bf16[12,64,1024]{2,1,0:T(8,128)(2,1)}, u32[]{:S(2)}) copy-start(bf16[12,64,1024]{2,1,0:T(8,128)(2,1)} %x_ref.1) | copy-start | bytes 4718596
  109.6 4.2 copy-start.36
  113.2 24.5 %copy-start.2 = (bf16[4,192,1024]{2,1,0:T(8,128)(2,1)}, bf16[4,192,1024]{2,1,0:T(8,128)(2,1)S(1)}, u32[]{:S(2)}) copy-start(bf16[4,192,1024]{2,1,0:T(8,128)(2,1)S(1)} %pair_sum_4.1) | copy-start | bytes 4718596
  113.8 1.8 copy-start.42
  115.6 5.5 %copy-start.20 = (bf16[12,64,1024]{2,1,0:T(8,128)(2,1)}, bf16[12,64,1024]{2,1,0:T(8,128)(2,1)S(1)}, u32[]{:S(2)}) copy-start(bf16[12,64,1024]{2,1,0:T(8,128)(2,1)S(1)} %multiply_convert_fusion.3) | copy-start | bytes 4718596
  115.6 2.6 copy-start.12
  115.6 2.9 copy-start.43
  126.5 2.6 copy-start.48
  126.5 2.6 copy-start.46
  135.4 3.6 copy-start.4
  137.8 1.3 copy-start.34
  139.1 2.0 copy-start.22
  186.0 8.3 %copy-start.8 = (bf16[3,1024,128]{2,1,0:T(8,128)(2,1)S(1)}, bf16[3,1024,128]{2,1,0:T(8,128)(2,1)}, u32[]{:S(2)}) copy-start(bf16[3,1024,128]{2,1,0:T(8,128)(2,1)} %get-tuple-element.46) | copy-start | bytes 2359300
  194.4 55.6 %copy-start.18 = (bf16[12,64,1024]{2,1,0:T(8,128)(2,1)S(1)}, bf16[12,64,1024]{2,1,0:T(8,128)(2,1)}, u32[]{:S(2)}) copy-start(bf16[12,64,1024]{2,1,0:T(8,128)(2,1)} %get-tuple-element.47) | copy-start | bytes 4718596
  194.4 55.6 %copy-start.26 = (bf16[12,64,48]{2,1,0:T(8,128)(2,1)S(1)}, bf16[12,64,48]{2,1,0:T(8,128)(2,1)}, u32[]{:S(2)}) copy-start(bf16[12,64,48]{2,1,0:T(8,128)(2,1)} %get-tuple-element.43) | copy-start | bytes 221188
  250.5 2.2 copy-start.15
  250.5 2.2 copy-start.27
  252.6 1.1 copy-start.29
  252.7 1.6 copy-start.32
  253.8 1.2 copy-start.33
  254.3 1.2 copy-start.25
  255.0 1.1 copy-start.24
  257.0 6.7 %copy-start.39 = (f32[12,64]{1,0:T(8,128)S(1)}, f32[12,64]{1,0:T(8,128)}, u32[]{:S(2)}) copy-start(f32[12,64]{1,0:T(8,128)} %get-tuple-element.58) | copy-start | bytes 9220
  257.1 7.8 %copy-start.10 = (bf16[12,64,1024]{2,1,0:T(8,128)(2,1)S(1)}, bf16[12,64,1024]{2,1,0:T(8,128)(2,1)}, u32[]{:S(2)}) copy-start(bf16[12,64,1024]{2,1,0:T(8,128)(2,1)} %x_ref.1) | copy-start | bytes 4718596
  257.1 7.8 %copy-start.38 = (f32[1024]{0:T(1024)S(1)}, f32[1024]{0:T(1024)}, u32[]{:S(2)}) copy-start(f32[1024]{0:T(1024)} %param.17) | copy-start | bytes 12292
  257.1 9.1 %copy-start.40 = (bf16[1024]{0:T(1024)(128)(2,1)S(1)}, bf16[1024]{0:T(1024)(128)(2,1)}, u32[]{:S(2)}) copy-start(bf16[1024]{0:T(1024)(128)(2,1)} %get-tuple-element.54) | copy-start | bytes 6148
  263.7 1.1 copy-start.6
  263.7 3.0 copy-start.19
  263.7 3.0 copy-start.31
  266.7 1.5 copy-start.21
  266.7 2.1 copy-start.47
  268.8 4.0 copy-start.49
  272.8 4.2 copy-start.23
  272.8 4.2 copy-start.45
  277.0 1.4 copy-start.13
  277.0 2.1 copy-start.50
  501.9 5.2 copy-start.17
  507.1 3.1 copy-start.16
  522.3 8.9 %copy-start.7 = (bf16[4,192,1024]{2,1,0:T(8,128)(2,1)S(1)}, bf16[4,192,1024]{2,1,0:T(8,128)(2,1)}, u32[]{:S(2)}) copy-start(bf16[4,192,1024]{2,1,0:T(8,128)(2,1)} %copy-done.6) | copy-start | bytes 4718596
  522.3 8.9 %copy-start.11 = (bf16[12,64,1024]{2,1,0:T(8,128)(2,1)S(1)}, bf16[12,64,1024]{2,1,0:T(8,128)(2,1)}, u32[]{:S(2)}) copy-start(bf16[12,64,1024]{2,1,0:T(8,128)(2,1)} %x_ref.1) | copy-start | bytes 4718596
  522.3 8.9 %copy-start.14 = (bf16[12,64,1024]{2,1,0:T(8,128)(2,1)S(1)}, bf16[12,64,1024]{2,1,0:T(8,128)(2,1)}, u32[]{:S(2)}) copy-start(bf16[12,64,1024]{2,1,0:T(8,128)(2,1)} %param.29) | copy-start | bytes 4718596
  522.3 8.9 %copy-start.35 = (f32[12,64]{1,0:T(8,128)S(1)}, f32[12,64]{1,0:T(8,128)}, u32[]{:S(2)}) copy-start(f32[12,64]{1,0:T(8,128)} %copy-done.34) | copy-start | bytes 9220
  522.3 8.9 %copy-start.37 = (f32[1024]{0:T(1024)S(1)}, f32[1024]{0:T(1024)}, u32[]{:S(2)}) copy-start(f32[1024]{0:T(1024)} %param.25) | copy-start | bytes 12292
  527.5 3.7 copy-start.3
  527.5 3.7 copy-start.5
  531.2 4.0 copy-start.1
